TPU v7x, 128 devices: a whole 4x4x4 slice. The times are simulated.
128 devices in a mesh: row: 16 (over y, x), col: 8 (over z, core).
Axes of the slice: x: 4, y: 4, z: 4, core: 2. Of those that a mesh axis runs over, the one named last changes fastest.
Arguments:
- audio: float32 [16384, 768], P(('row', 'col')), may hold values from -80 to 80, as said below
- video: float32 [16384, 768], P(('col', 'row')), may hold values from -80 to 80, as said below
Outputs:
- loss: float32 [], replicated
- audio_grad: float32 [16384, 768], P(('row', 'col'))
- video_grad: float32 [16384, 768], P(('col', 'row'))
Inputs may be any that keep to these rules, and one draw needn't show every extreme that they name: audio embeddings, float32. video embeddings, float32.
All inputs are finite; a program needn't handle non-finite values.
Results may differ from a plain program's by a relative error of at most 0.0014.
Values sent between devices are 32-bit elements; how exact they have to be, the bound alone decides.
No kernel may reach another device: no remote copies, remote signals or barrier semaphores. Data moves between devices by JAX's collectives and lax.ppermute only.
A program may use at most 128 MiB of HBM per device.

v0:
```python
import jax
import jax.numpy as jnp
from jax import lax
from jax.sharding import PartitionSpec as P

ITERS = 3


HIGH = lax.Precision.HIGHEST


def unit_rows(values):
    inv = lax.rsqrt(jnp.sum(values * values, axis=1, keepdims=True) + 1e-06)
    return (values * inv, inv)


def local(audio, video):
    block = audio.shape[0]
    count = block * lax.axis_size("row") * lax.axis_size("col")
    audio_unit, audio_inv = unit_rows(audio)
    video_unit, video_inv = unit_rows(video)
    audio_tile = lax.all_gather(audio_unit, "col", axis=0, tiled=True)
    video_tile = lax.all_gather(video_unit, "row", axis=0, tiled=True)
    scores = 20.0 * jnp.dot(
        audio_tile, video_tile.T, precision=HIGH, preferred_element_type=jnp.float32
    )
    kernel = jnp.exp(scores)
    totals = lax.psum(jnp.sum(kernel, axis=1), "col")
    col_scale = jnp.ones((kernel.shape[1],), jnp.float32)
    row_scale = jnp.ones((kernel.shape[0],), jnp.float32)
    for step in range(ITERS):
        row_sums = lax.psum(jnp.sum(kernel * col_scale[None, :], axis=1), "col")
        row_scale = 1.0 / row_sums
        col_sums = lax.psum(jnp.sum(kernel * row_scale[:, None], axis=0), "row")
        col_scale = 1.0 / col_sums
    target = kernel * row_scale[:, None] * col_scale[None, :]
    target_rows = lax.psum(jnp.sum(target, axis=1), "col")
    local_loss = jnp.sum(target * (scores - jnp.log(totals)[:, None]))
    loss = -lax.psum(local_loss, ("row", "col")) / count
    score_grad = ((target_rows / totals)[:, None] * kernel - target) / count
    full_audio = lax.psum(
        20.0 * jnp.dot(score_grad, video_tile, precision=HIGH, preferred_element_type=jnp.float32),
        "col",
    )
    full_video = lax.psum(
        20.0
        * jnp.dot(score_grad.T, audio_tile, precision=HIGH, preferred_element_type=jnp.float32),
        "row",
    )
    unit_audio = lax.dynamic_slice_in_dim(full_audio, lax.axis_index("col") * block, block, 0)
    unit_video = lax.dynamic_slice_in_dim(full_video, lax.axis_index("row") * block, block, 0)
    audio_grad = (
        unit_audio - audio_unit * jnp.sum(audio_unit * unit_audio, axis=1, keepdims=True)
    ) * audio_inv
    video_grad = (
        unit_video - video_unit * jnp.sum(video_unit * unit_video, axis=1, keepdims=True)
    ) * video_inv
    return (loss, audio_grad, video_grad)


def solution(mesh):
    in_specs = (P(("row", "col"), None), P(("col", "row"), None))
    out_specs = (P(), P(("row", "col"), None), P(("col", "row"), None))
    return jax.shard_map(local, mesh=mesh, in_specs=in_specs, out_specs=out_specs, check_vma=False)
```

profile of v0, /device:TPU:0, one launch (start us, length us, event | category | flops | bytes accessed | tf_op | source)
XLA Modules:
  0.0 552.3 jit_solution(12722929974929698216)
XLA Ops:
  8.3 1.8 broadcast_multiply_fusion.1
  11.4 1.8 broadcast_multiply_fusion
  13.3 27.5 %all-gather.3.cloned.1.call-done = f32[1024,768]{1,0:T(8,128)} async-done(((f32[128,768]{1,0:T(8,128)}), f32[1024,768]{1,0:T(8,128)}) %all-gather.3.cloned.1.call-update) | async-done | bytes 3145744 | tf_op jit(solution)/shard_map/all_gather | solution.py:22
  40.8 63.8 %all-gather.5.cloned.1.call-done = f32[2048,768]{1,0:T(8,128)} async-done(((f32[128,768]{1,0:T(8,128)}), f32[2048,768]{1,0:T(8,128)}) %all-gather.5.cloned.1.call-update) | async-done | bytes 6291472 | tf_op jit(solution)/shard_map/all_gather | solution.py:23
  104.6 25.6 %exponential_reduce_fusion = (f32[1024]{0:T(1024)S(1)}, f32[1024,2048]{1,0:T(8,128)}) fusion(f32[1024,768]{1,0:T(8,128)} %all-gather.3.cloned.1.call-done, f32[2048,768]{1,0:T(8,128)} %all-gather.5.cloned.1.call-done), kind=kOutput, calls=%fused_computation.9 | convolution fusion | flops 19331547136 | bytes 17829888 | tf_op jit(solution)/shard_map/dot_general | solution.py:24
  130.2 14.9 %psum.73 = f32[1024]{0:T(1024)S(1)} all-reduce(f32[1024]{0:T(1024)S(1)} %get-tuple-element.7), channel_id=1, replica_groups=mesh['row'=16,'col'=8] {'col'}, use_global_device_ids=true, to_apply=%region_3.0 | all-reduce | flops 1024 | bytes 8192 | tf_op jit(solution)/shard_map/psum | solution.py:32
  145.2 4.5 multiply_reduce_fusion.4
  149.7 39.0 %psum.74 = f32[2048]{0:T(1024)S(1)} all-reduce(f32[2048]{0:T(1024)S(1)} %multiply_reduce_fusion.4), channel_id=1, replica_groups=mesh['row'=16,'col'=8] {'row'}, use_global_device_ids=true, to_apply=%region_5.0 | all-reduce | flops 2048 | bytes 16384 | tf_op jit(solution)/shard_map/psum | solution.py:34
  188.7 4.7 multiply_reduce_fusion.3
  193.4 12.4 %psum.75 = f32[1024]{0:T(1024)S(1)} all-reduce(f32[1024]{0:T(1024)S(1)} %multiply_reduce_fusion.3), channel_id=1, replica_groups=mesh['row'=16,'col'=8] {'col'}, use_global_device_ids=true, to_apply=%region_7.0 | all-reduce | flops 1024 | bytes 8192 | tf_op jit(solution)/shard_map/psum | solution.py:32
  205.9 4.5 multiply_reduce_fusion.2
  210.4 36.0 %psum.76 = f32[2048]{0:T(1024)S(1)} all-reduce(f32[2048]{0:T(1024)S(1)} %multiply_reduce_fusion.2), channel_id=1, replica_groups=mesh['row'=16,'col'=8] {'row'}, use_global_device_ids=true, to_apply=%region_9.0 | all-reduce | flops 2048 | bytes 16384 | tf_op jit(solution)/shard_map/psum | solution.py:34
  246.4 4.7 multiply_reduce_fusion.1
  251.1 12.4 %psum.77 = f32[1024]{0:T(1024)S(1)} all-reduce(f32[1024]{0:T(1024)S(1)} %multiply_reduce_fusion.1), channel_id=1, replica_groups=mesh['row'=16,'col'=8] {'col'}, use_global_device_ids=true, to_apply=%region_11.0 | all-reduce | flops 1024 | bytes 8192 | tf_op jit(solution)/shard_map/psum | solution.py:32
  263.5 4.5 multiply_reduce_fusion.5
  268.0 38.0 %psum.78 = f32[2048]{0:T(1024)S(1)} all-reduce(f32[2048]{0:T(1024)S(1)} %multiply_reduce_fusion.5), channel_id=1, replica_groups=mesh['row'=16,'col'=8] {'row'}, use_global_device_ids=true, to_apply=%region_13.0 | all-reduce | flops 2048 | bytes 16384 | tf_op jit(solution)/shard_map/psum | solution.py:34
  306.1 7.1 %fusion = (f32[1024]{0:T(1024)S(1)}, f32[]{:T(128)}) fusion(f32[1024,2048]{1,0:T(8,128)} %get-tuple-element.8, f32[2048]{0:T(1024)S(1)} %broadcast_divide_fusion, f32[1024]{0:T(1024)S(1)} %broadcast_divide_fusion.3, f32[1024]{0:T(1024)S(1)} %get-tuple-element.5), kind=kLoop, calls=%fused_computation.8 | loop fusion | flops 12581887 | bytes 8409092 | tf_op jit(solution)/shard_map/reduce_sum | solution.py:37
  313.2 12.4 %psum.80 = f32[1024]{0:T(1024)S(1)} all-reduce(f32[1024]{0:T(1024)S(1)} %get-tuple-element.3), channel_id=1, replica_groups=mesh['row'=16,'col'=8] {'col'}, use_global_device_ids=true, to_apply=%region_17.0 | all-reduce | flops 1024 | bytes 8192 | tf_op jit(solution)/shard_map/psum | solution.py:37
  325.6 26.9 %fusion.12 = f32[1024,768]{1,0:T(8,128)} fusion(f32[2048,768]{1,0:T(8,128)} %all-gather.5.cloned.1.call-done, f32[1024,2048]{1,0:T(8,128)} %get-tuple-element.8, f32[1024]{0:T(1024)S(1)} %div.37, f32[2048]{0:T(1024)S(1)} %broadcast_divide_fusion, f32[1024]{0:T(1024)S(1)} %broadcast_divide_fusion.3), kind=kOutput, calls=%fused_computation.22 | convolution fusion | flops 19338625024 | bytes 17842176 | tf_op jit(solution)/shard_map/dot_general | solution.py:42
  352.8 27.7 %fusion.11 = f32[2048,768]{1,0:T(8,128)} fusion(f32[1024,768]{1,0:T(8,128)} %all-gather.3.cloned.1.call-done, f32[1024,2048]{1,0:T(8,128)} %get-tuple-element.8, f32[1024]{0:T(1024)S(1)} %div.37, f32[2048]{0:T(1024)S(1)} %broadcast_divide_fusion, f32[1024]{0:T(1024)S(1)} %broadcast_divide_fusion.3), kind=kOutput, calls=%fused_computation.21 | convolution fusion | flops 19339411456 | bytes 17842176 | tf_op jit(solution)/shard_map/dot_general | solution.py:47
  380.6 63.5 %psum.79 = f32[]{:T(128)} all-reduce(f32[]{:T(128)} %get-tuple-element.4), channel_id=1, replica_groups=mesh['row'=16,'col'=8] {'row','col'}, use_global_device_ids=true, to_apply=%region_15.0 | all-reduce | flops 1 | bytes 8 | tf_op jit(solution)/shard_map/psum | solution.py:39
  446.0 1.9 subtract_multiply_fusion.8
  447.9 93.3 %all-reduce.5.cloned.1.call-done = f32[2048,768]{1,0:T(8,128)} async-done(((f32[2048,768]{1,0:T(8,128)}), f32[2048,768]{1,0:T(8,128)}) %all-reduce.5.cloned.1.call-update) | async-done | bytes 6291472 | tf_op jit(solution)/shard_map/psum | solution.py:45
  542.4 1.9 subtract_multiply_fusion.7
  (26 shorter events, 5.1 us)
Async XLA Ops:
  7.2 33.6 %all-gather.3.cloned.1.call-start = ((), (), s32[]{:S(2)}) async-start(), calls=%async_computation | async-start | bytes 3538944 | tf_op jit(solution)/shard_map/all_gather | solution.py:22
  10.2 94.4 %all-gather.5.cloned.1.call-start = ((), (), s32[]{:S(2)}) async-start(), calls=%async_computation.1 | async-start | bytes 6684672 | tf_op jit(solution)/shard_map/all_gather | solution.py:23
  13.2 431.5 %all-reduce.3.cloned.1.call-start = ((), (), s32[]{:S(2)}) async-start(), calls=%async_computation.2 | async-start | bytes 6291456 | tf_op jit(solution)/shard_map/psum | solution.py:41
  352.5 92.2 %copy-start = (f32[128,768]{1,0:T(8,128)S(1)}, f32[128,768]{1,0:T(8,128)}, u32[]{:S(2)}) copy-start(f32[128,768]{1,0:T(8,128)} %param.2) | copy-start | bytes 1179652
  352.5 188.7 %all-reduce.5.cloned.1.call-start = ((), (), s32[]{:S(2)}) async-start(), calls=%async_computation.3 | async-start | bytes 12582912 | tf_op jit(solution)/shard_map/psum | solution.py:45
  380.5 160.7 %copy-start.1 = (f32[128,768]{1,0:T(8,128)S(1)}, f32[128,768]{1,0:T(8,128)}, u32[]{:S(2)}) copy-start(f32[128,768]{1,0:T(8,128)} %param.3) | copy-start | bytes 1179652
Sparse Core Ops, SparseCore 0:
  10.3 30.4 all-gather.2
  43.5 61.0 all-gather.4
  352.6 62.7 all-reduce.2
  418.8 122.4 all-reduce.4
where the time goes:
time: 562 us; the launch traced here: 552 us
  blocking collectives  229 us (41%)
  waiting for transfers between devices  185 us (33%)
  matrix products  80.2 us (14%)
  other arithmetic  42.2 us (8%)
  between operations  16.1 us (3%)
    psum x3, blocking collectives, local(): col_sums = lax.psum(jnp.sum(kernel * row_scale[:, None], axis=0), 'row')  113 us
    psum x1, waiting for transfers between devices, local(): lax.psum(20.0 * jnp.dot(score_grad.T, audio_tile, precision=HIGH, preferr...  93.3 us
    all_gather x1, waiting for transfers between devices, local(): video_tile = lax.all_gather(video_unit, 'row', axis=0, tiled=True)  63.8 us
    psum x1, blocking collectives, local(): loss = -lax.psum(local_loss, ('row', 'col')) / count  63.5 us
    psum x3, blocking collectives, local(): row_sums = lax.psum(jnp.sum(kernel * col_scale[None, :], axis=1), 'col')  39.8 us
    dot_general x1, matrix products, local(): jnp.dot(score_grad.T, audio_tile, precision=HIGH, preferred_element_type=...  27.7 us
    all_gather x1, waiting for transfers between devices, local(): audio_tile = lax.all_gather(audio_unit, 'col', axis=0, tiled=True)  27.5 us
    dot_general x1, matrix products, local(): jnp.dot(score_grad, video_tile, precision=HIGH, preferred_element_type=jn...  26.9 us
  transfers between devices with their start and end apart: 4, of which 3 were waited for; matrix products, arithmetic and copies ran while one was open for 6% of the time, Pallas kernels for 0%

commit v1 on v0

v1 whole, which is shorter than its diff:
```python
import jax
import jax.numpy as jnp
from jax import lax
from jax.experimental import pallas as pl
from jax.experimental.pallas import tpu as pltpu
from jax.sharding import PartitionSpec as P

ITERS = 3
F32 = jnp.float32
BF16 = jnp.bfloat16
VMEM_BYTES = 56 * 1024 * 1024
ORDER = (0, -1, 1, 2)


def params(limit=VMEM_BYTES, **kw):
    return pltpu.CompilerParams(vmem_limit_bytes=limit, **kw)


def vmem():
    return pl.BlockSpec(memory_space=pltpu.VMEM)


def smem():
    return pl.BlockSpec(memory_space=pltpu.SMEM)


def split(value):
    high = value.astype(BF16)
    return high, (value - high.astype(F32)).astype(BF16)


def dot3(lhs, rhs, dims):
    (lh, ll), (rh, rl) = lhs, rhs
    dot = lambda p, q: lax.dot_general(p, q, (dims, ((), ())), preferred_element_type=F32)
    return dot(lh, rh) + (dot(lh, rl) + dot(ll, rh))


def unit_kernel(a_ref, v_ref, au_ref, vu_ref, ai_ref, vi_ref):
    for src, dst, inv_ref in ((a_ref, au_ref, ai_ref), (v_ref, vu_ref, vi_ref)):
        x = src[...]
        inv = lax.rsqrt(jnp.sum(x * x, axis=1, keepdims=True) + 1e-06)
        dst[...] = x * inv
        inv_ref[...] = jnp.broadcast_to(inv, inv_ref.shape)


def unit_rows(audio, video):
    n, d = audio.shape
    return pl.pallas_call(
        unit_kernel,
        out_shape=[jax.ShapeDtypeStruct((n, d), F32)] * 2 + [jax.ShapeDtypeStruct((n, 128), F32)] * 2,
        in_specs=[vmem()] * 2,
        out_specs=[vmem()] * 4,
        compiler_params=params(),
        name="unit_rows",
    )(audio, video)


def scores_kernel(pos_ref, a_ref, *refs):
    pieces, (kt_ref, ah_ref, al_ref, vh_ref, vl_ref, sum_ref) = refs[:8], refs[8:]
    ah, al = split(a_ref[...])
    ah_ref[...] = ah
    al_ref[...] = al
    total = jnp.zeros((8, a_ref.shape[0]), F32)
    for p, piece in enumerate(pieces):
        vh, vl = split(piece[...])
        s = dot3((vh, vl), (ah_ref[...], al_ref[...]), ((1,), (1,)))
        k = jnp.exp(20.0 * s)
        total = total + jnp.sum(k.reshape(32, 8, -1), axis=0)
        half, j = p // 4, p % 4
        major = (pos_ref[half] + ORDER[j] + 4) % 4
        for b in range(4):
            minor = (pos_ref[1 - half] + ORDER[b] + 4) % 4
            at = pl.ds(pl.multiple_of(half * 1024 + major * 256 + minor * 64, 64), 64)
            rows = slice(b * 64, b * 64 + 64)
            kt_ref[at, :] = k[rows]
            vh_ref[at, :] = vh[rows]
            vl_ref[at, :] = vl[rows]
    put_lanes(sum_ref, jnp.sum(total, axis=0, keepdims=True))


def put_lanes(ref, row):
    copies, chunks, _ = ref.shape
    for m in range(chunks):
        part = row[:, m * 128 : m * 128 + 128]
        for d in range(copies):
            ref[d, m : m + 1, :] = part


def scores(pos, audio_tile, pieces):
    n, d = audio_tile.shape
    m = 2048
    return pl.pallas_call(
        scores_kernel,
        out_shape=[
            jax.ShapeDtypeStruct((m, n), F32),
            jax.ShapeDtypeStruct((n, d), BF16),
            jax.ShapeDtypeStruct((n, d), BF16),
            jax.ShapeDtypeStruct((m, d), BF16),
            jax.ShapeDtypeStruct((m, d), BF16),
            jax.ShapeDtypeStruct((8, 8, 128), F32),
        ],
        in_specs=[smem()] + [vmem()] * 9,
        out_specs=[vmem()] * 6,
        compiler_params=params(),
        name="scores",
    )(pos, audio_tile, *pieces)


def scale_of(part_ref):
    return 1.0 / jnp.sum(part_ref[...], axis=0)


def columns_kernel(part_ref, kt_ref, out_ref):
    r = scale_of(part_ref)
    k = pl.program_id(0)
    for b in range(2):
        acc = jnp.zeros((128, 128), F32)
        for m in range(8):
            acc = acc + kt_ref[b * 128 : b * 128 + 128, m * 128 : m * 128 + 128] * r[m : m + 1, :]
        row = jnp.sum(acc.T, axis=0, keepdims=True)
        for d in range(16):
            out_ref[d, pl.ds(k * 2 + b, 1), :] = row


def rows_kernel(part_ref, kt_ref, out_ref, scale_ref, acc_ref):
    k = pl.program_id(0)

    @pl.when(k == 0)
    def _():
        scale_ref[...] = scale_of(part_ref)
        acc_ref[...] = jnp.zeros_like(acc_ref)

    for b in range(2):
        c = jnp.broadcast_to(scale_ref[pl.ds(k * 2 + b, 1), :], (128, 128)).T
        for m in range(8):
            lanes = slice(m * 128, m * 128 + 128)
            prod = kt_ref[b * 128 : b * 128 + 128, lanes] * c
            acc_ref[:, lanes] += jnp.sum(prod.reshape(16, 8, 128), axis=0)

    @pl.when(k == 7)
    def _():
        put_lanes(out_ref, jnp.sum(acc_ref[...], axis=0, keepdims=True))


def whole(shape):
    return pl.BlockSpec(shape, lambda k: (0,) * len(shape))


def columns_pass(part, kt):
    return pl.pallas_call(
        columns_kernel,
        grid=(8,),
        out_shape=jax.ShapeDtypeStruct((16, 16, 128), F32),
        in_specs=[whole((8, 8, 128)), pl.BlockSpec((256, 1024), lambda k: (k, 0))],
        out_specs=whole((16, 16, 128)),
        compiler_params=params(),
        name="column_sums",
    )(part, kt)


def rows_pass(part, kt):
    return pl.pallas_call(
        rows_kernel,
        grid=(8,),
        out_shape=jax.ShapeDtypeStruct((8, 8, 128), F32),
        in_specs=[whole((16, 16, 128)), pl.BlockSpec((256, 1024), lambda k: (k, 0))],
        out_specs=whole((8, 8, 128)),
        scratch_shapes=[pltpu.VMEM((16, 128), F32), pltpu.VMEM((8, 1024), F32)],
        compiler_params=params(),
        name="row_sums",
    )(part, kt)


def grads_kernel(count, tot_ref, rp_ref, cp_ref, tp_ref, kt_ref, ah_ref, al_ref, vh_ref, vl_ref,
                 y_ref, u_ref, loss_ref, c_ref, r_ref, w_ref, log_ref):
    k = pl.program_id(0)

    @pl.when(k == 0)
    def _():
        c_ref[...] = scale_of(cp_ref)
        totals = jnp.sum(tot_ref[...], axis=0)
        r = scale_of(rp_ref)
        w = r * jnp.sum(tp_ref[...], axis=0) / totals
        logs = jnp.log(totals)
        for m in range(8):
            lanes = slice(m * 128, m * 128 + 128)
            r_ref[:, lanes] = jnp.broadcast_to(r[m : m + 1], (8, 128))
            w_ref[:, lanes] = jnp.broadcast_to(w[m : m + 1], (8, 128))
            log_ref[:, lanes] = jnp.broadcast_to(logs[m : m + 1], (8, 128))
        u_ref[...] = jnp.zeros_like(u_ref)
        loss_ref[...] = jnp.zeros_like(loss_ref)

    c = jnp.concatenate(
        [jnp.broadcast_to(c_ref[pl.ds(k * 2 + b, 1), :], (128, 128)).T for b in range(2)], axis=0
    )
    c = jnp.concatenate([c] * 8, axis=1)
    kernel = kt_ref[...]
    scaled = r_ref[0:1, :] * c
    g = kernel * ((w_ref[0:1, :] - scaled) * (20.0 / count))
    terms = kernel * scaled * (jnp.log(kernel) - log_ref[0:1, :])
    terms = jnp.sum(terms.reshape(32, 8, 1024), axis=0)
    loss_ref[...] += sum(terms[:, m * 128 : m * 128 + 128] for m in range(8))
    g = split(g)
    y_ref[...] = dot3(g, (ah_ref[...], al_ref[...]), ((1,), (0,)))
    u_ref[...] += dot3(g, (vh_ref[...], vl_ref[...]), ((0,), (0,)))


def grads(count, tot, rpart, cpart, tpart, kt, ah, al, vh, vl):
    vec = whole((8, 8, 128))
    return pl.pallas_call(
        lambda *refs: grads_kernel(count, *refs),
        grid=(8,),
        out_shape=[
            jax.ShapeDtypeStruct((2048, 768), F32),
            jax.ShapeDtypeStruct((1024, 768), F32),
            jax.ShapeDtypeStruct((8, 128), F32),
        ],
        in_specs=[
            vec, vec, whole((16, 16, 128)), vec,
            pl.BlockSpec((256, 1024), lambda k: (k, 0)),
            whole((1024, 768)), whole((1024, 768)),
            pl.BlockSpec((256, 768), lambda k: (k, 0)),
            pl.BlockSpec((256, 768), lambda k: (k, 0)),
        ],
        out_specs=[
            pl.BlockSpec((256, 768), lambda k: (k, 0)),
            whole((1024, 768)),
            whole((8, 128)),
        ],
        scratch_shapes=[pltpu.VMEM((16, 128), F32)] + [pltpu.VMEM((8, 1024), F32)] * 3,
        compiler_params=params(),
        name="unit_grads",
    )(tot, rpart, cpart, tpart, kt, ah, al, vh, vl)


def step_y(v, k):
    return lax.ppermute(v, "row", [(i, ((i // 4 + k) % 4) * 4 + i % 4) for i in range(16)])


def step_x(v, k):
    return lax.ppermute(v, "row", [(i, (i // 4) * 4 + (i % 4 + k) % 4) for i in range(16)])


def ring_gather(step, v):
    half = v.shape[0] // 2
    left, right = step(v, 1), step(v, -1)
    far = jnp.concatenate([step(left[:half], 1), step(right[half:], -1)], axis=0)
    return [v, left, right, far]


def gather_video(v):
    half = v.shape[0] // 2
    first = jnp.concatenate(ring_gather(step_x, v[:half]), axis=0)
    second = jnp.concatenate(ring_gather(step_y, v[half:]), axis=0)
    return ring_gather(step_y, first) + ring_gather(step_x, second)


def ring_scatter(step, v, me):
    size = v.shape[0] // 4
    half = size // 2
    block = lambda k: lax.dynamic_slice_in_dim(v, ((me + k) % 4) * size, size, 0)
    far = block(2)
    from_left, from_right = step(far[:half], 1), step(far[half:], -1)
    up, down = block(1), block(3)
    up = jnp.concatenate([up[:half] + from_left, up[half:]], axis=0)
    down = jnp.concatenate([down[:half], down[half:] + from_right], axis=0)
    return block(0) + step(up, 1) + step(down, -1)


def scatter_video(v, y, x):
    half = v.shape[0] // 2
    first = ring_scatter(step_x, ring_scatter(step_y, v[:half], y), x)
    second = ring_scatter(step_y, ring_scatter(step_x, v[half:], x), y)
    return jnp.concatenate([first, second], axis=0)


def swap(part, axis):
    return lax.all_to_all(part, axis, 0, 0, tiled=True)


def local(audio, video):
    count = audio.shape[0] * 128
    row = lax.axis_index("row")
    y, x = row // 4, row % 4
    pos = jnp.stack([y, x]).astype(jnp.int32)
    audio_unit, video_unit, audio_inv, video_inv = unit_rows(audio, video)
    audio_tile = lax.all_gather(audio_unit, "col", axis=0, tiled=True)
    pieces = gather_video(video_unit)
    kt, ah, al, vh, vl, part = scores(pos, audio_tile, pieces)
    totals = swap(part, "col")
    rpart = totals
    for step in range(ITERS):
        cpart = swap(columns_pass(rpart, kt), "row")
        part = swap(rows_pass(cpart, kt), "col")
        if step < ITERS - 1:
            rpart = part
    full_video, full_audio, terms = grads(count, totals, rpart, cpart, part, kt, ah, al, vh, vl)
    terms = jnp.sum(swap(jnp.broadcast_to(terms[None], (8, 8, 128)), "col"), axis=0)
    terms = swap(jnp.broadcast_to(terms[None], (16, 8, 128)), "row")
    loss = -jnp.sum(terms) / count
    unit_audio = lax.psum_scatter(full_audio, "col", scatter_dimension=0, tiled=True)
    unit_video = scatter_video(full_video, y, x)

    def project(unit, grad, inv):
        return (grad - unit * jnp.sum(unit * grad, axis=1, keepdims=True)) * inv[:, :1]

    return (
        loss,
        project(audio_unit, unit_audio, audio_inv),
        project(video_unit, unit_video, video_inv),
    )


def solution(mesh):
    in_specs = (P(("row", "col"), None), P(("col", "row"), None))
    out_specs = (P(), P(("row", "col"), None), P(("col", "row"), None))
    return jax.shard_map(local, mesh=mesh, in_specs=in_specs, out_specs=out_specs, check_vma=False)
```

time: 562 us -> 322 us (0.57); the launches traced: 552 us -> 320 us
  blocking collectives: 229 us -> 75.8 us
  waiting for transfers between devices: 185 us -> 50 us
  Pallas kernels: 0 us -> 91.5 us
  matrix products: 80.2 us -> 0 us
  starting transfers between devices: 0.38 us -> 57.1 us
  other arithmetic: 42.2 us -> 18.5 us
  local copies, waits for them, and re-layouts: 0.01 us -> 11 us
    psum x8 -> x0, blocking collectives: 229 us -> none  [the longest x3 113 us: local(): col_sums = lax.psum(jnp.sum(kernel * row_scale[:, None], axis=0), 'row')]
    psum x2 -> x0, waiting for transfers between devices: 93.4 us -> none  [the longest x1 93.3 us: local(): lax.psum(20.0 * jnp.dot(score_grad.T, audio_tile, precision=HIGH, preferr...]
    pallas_call x0 -> x9, Pallas kernels: none -> 91.5 us  [the longest x1 28.8 us: grads(): pl.pallas_call(lambda *refs: grads_kernel(count, *refs), grid=(8,), out_s...]
    dot_general x3 -> x0, matrix products: 80.2 us -> none  [the longest x1 27.7 us: local(): jnp.dot(score_grad.T, audio_tile, precision=HIGH, preferred_element_type=...]
    all_to_all x0 -> x7, blocking collectives: none -> 75.8 us  [swap(): return lax.all_to_all(part, axis, 0, 0, tiled=True)]
    all_gather x1 -> x0, waiting for transfers between devices: 63.8 us -> none  [local(): video_tile = lax.all_gather(video_unit, 'row', axis=0, tiled=True)]
    ppermute x0 -> x32, starting transfers between devices: none -> 47.6 us  [the longest x16 24.9 us: step_y(): lax.ppermute(v, 'row', [(i, (i // 4 + k) % 4 * 4 + i % 4) for i in range(...]
    ppermute x0 -> x32, waiting for transfers between devices: none -> 37.1 us  [the longest x16 20.6 us: step_y(): lax.ppermute(v, 'row', [(i, (i // 4 + k) % 4 * 4 + i % 4) for i in range(...]
  transfers between devices with their start and end apart: 4 -> 36, of which waited for: 3 -> 12; matrix products, arithmetic and copies ran while one was open for 6% -> 8% of each run, Pallas kernels for 0% -> 0%
where the time goes in v1:
time: 322 us; the launch traced here: 320 us
  Pallas kernels  91.5 us (28%)
  blocking collectives  75.8 us (24%)
  starting transfers between devices  57.1 us (18%)
  waiting for transfers between devices  50 us (16%)
  other arithmetic  18.5 us (6%)
  between operations  16.4 us (5%)
  local copies, waits for them, and re-layouts  11 us (3%)
    all_to_all x7, blocking collectives, swap(): return lax.all_to_all(part, axis, 0, 0, tiled=True)  75.8 us
    pallas_call x1, Pallas kernels, grads(): pl.pallas_call(lambda *refs: grads_kernel(count, *refs), grid=(8,), out_s...  28.8 us
    ppermute x16, starting transfers between devices, step_y(): lax.ppermute(v, 'row', [(i, (i // 4 + k) % 4 * 4 + i % 4) for i in range(...  24.9 us
    ppermute x16, starting transfers between devices, step_x(): lax.ppermute(v, 'row', [(i, i // 4 * 4 + (i % 4 + k) % 4) for i in range(...  22.7 us
    ppermute x16, waiting for transfers between devices, step_y(): lax.ppermute(v, 'row', [(i, (i // 4 + k) % 4 * 4 + i % 4) for i in range(...  20.6 us
    pallas_call x3, Pallas kernels, columns_pass(): pl.pallas_call(columns_kernel, grid=(8,), out_shape=jax.ShapeDtypeStruct(...  20.4 us
    pallas_call x3, Pallas kernels, rows_pass(): pl.pallas_call(rows_kernel, grid=(8,), out_shape=jax.ShapeDtypeStruct((8,...  20.1 us
    pallas_call x1, Pallas kernels, scores(): pl.pallas_call(scores_kernel, out_shape=[jax.ShapeDtypeStruct((m, n), F32...  20.1 us
  transfers between devices with their start and end apart: 36, of which 12 were waited for; matrix products, arithmetic and copies ran while one was open for 8% of the time, Pallas kernels for 0%

profile of v1, /device:TPU:0, one launch (start us, length us, event | category | flops | bytes accessed | tf_op | source)
XLA Modules:
  0.0 320.2 jit_solution(6489336076689020779)
XLA Ops:
  17.9 3.8 %collective-permute-start.11 = (f32[32,768]{1,0:T(8,128)S(1)}, f32[32,768]{1,0:T(8,128)S(1)}, u32[]{:S(2)}, u32[]{:S(2)}) collective-permute-start(f32[32,768]{1,0:T(8,128)S(1)} %slice.157), channel_id=1, source_target_pairs={{0,96},{8,104},{16,112},{24,120},{32,0},{40,8},{48,16},{56,24},{64... | collective-permute-start | bytes 294920 | tf_op jit(solution)/shard_map/ppermute | solution.py:237
  24.8 5.7 %collective-permute-done.2 = f32[32,768]{1,0:T(8,128)S(1)} collective-permute-done((f32[32,768]{1,0:T(8,128)S(1)}, f32[32,768]{1,0:T(8,128)S(1)}, u32[]{:S(2)}, u32[]{:S(2)}) %collective-permute-start.2) | collective-permute-done | bytes 98336 | tf_op jit(solution)/shard_map/ppermute | solution.py:241
  36.0 12.2 %collective-permute-done.5.refs_2_ = f32[256,768]{1,0:T(8,128)S(1)} collective-permute-done((f32[256,768]{1,0:T(8,128)S(1)}, f32[256,768]{1,0:T(8,128)S(1)}, u32[]{:S(2)}, u32[]{:S(2)}) %collective-permute-start.5) | collective-permute-done | bytes 786464 | tf_op jit(solution)/shard_map/ppermute | solution.py:237
  57.2 4.8 %collective-permute-done.6 = f32[128,768]{1,0:T(8,128)} collective-permute-done((f32[128,768]{1,0:T(8,128)}, f32[128,768]{1,0:T(8,128)}, u32[]{:S(2)}, u32[]{:S(2)}) %collective-permute-start.6) | collective-permute-done | bytes 393248 | tf_op jit(solution)/shard_map/ppermute | solution.py:237
  66.3 20.1 %scores.1 = (f32[2048,1024]{1,0:T(8,128)}, bf16[1024,768]{1,0:T(8,128)(2,1)}, bf16[1024,768]{1,0:T(8,128)(2,1)}, bf16[2048,768]{1,0:T(8,128)(2,1)}, bf16[2048,768]{1,0:T(8,128)(2,1)}, /*index=5*/f32[8,8,128]{2,1,0:T(8,128)}) custom-call(s32[2]{0:T(128)} %pad_add_fusion.pos_ref, f32[1024,768]{1,0:T(8,128)} %all-gather.2.cloned.1.call-done.a_ref, ...), custom_call_target="tpu_custom_call" | custom-call | tf_op jit(solution)/shard_map/scores/pallas_call | solution.py:92
  86.3 10.6 %all_to_all.45.part_ref.refs_0_ = f32[8,8,128]{2,1,0:T(8,128)} all-to-all(f32[8,8,128]{2,1,0:T(8,128)} %get-tuple-element.18), channel_id=1, replica_groups=mesh['row'=16,'col'=8] {'col'}, dimensions={0} | all-to-all | bytes 65536 | tf_op jit(solution)/shard_map/all_to_all | solution.py:278
  97.0 6.8 %column_sums.3 = f32[16,16,128]{2,1,0:T(8,128)} custom-call(f32[8,8,128]{2,1,0:T(8,128)} %all_to_all.45.part_ref.refs_0_, f32[2048,1024]{1,0:T(8,128)} %get-tuple-element.19.kt_ref.refs_4_), custom_call_target="tpu_custom_call" | custom-call | tf_op jit(solution)/shard_map/column_sums/pallas_call | solution.py:150
  103.8 12.7 %all_to_all.46.part_ref = f32[16,16,128]{2,1,0:T(8,128)} all-to-all(f32[16,16,128]{2,1,0:T(8,128)} %column_sums.3), channel_id=1, replica_groups=mesh['row'=16,'col'=8] {'row'}, dimensions={0} | all-to-all | bytes 262144 | tf_op jit(solution)/shard_map/all_to_all | solution.py:278
  116.5 6.7 %row_sums.3 = f32[8,8,128]{2,1,0:T(8,128)} custom-call(f32[16,16,128]{2,1,0:T(8,128)} %all_to_all.46.part_ref, f32[2048,1024]{1,0:T(8,128)} %get-tuple-element.19.kt_ref.refs_4_), custom_call_target="tpu_custom_call" | custom-call | tf_op jit(solution)/shard_map/row_sums/pallas_call | solution.py:162
  123.2 9.4 %all_to_all.47.part_ref = f32[8,8,128]{2,1,0:T(8,128)} all-to-all(f32[8,8,128]{2,1,0:T(8,128)} %row_sums.3), channel_id=1, replica_groups=mesh['row'=16,'col'=8] {'col'}, dimensions={0} | all-to-all | bytes 65536 | tf_op jit(solution)/shard_map/all_to_all | solution.py:278
  132.6 6.8 %column_sums.4 = f32[16,16,128]{2,1,0:T(8,128)} custom-call(f32[8,8,128]{2,1,0:T(8,128)} %all_to_all.47.part_ref, f32[2048,1024]{1,0:T(8,128)} %get-tuple-element.19.kt_ref.refs_4_), custom_call_target="tpu_custom_call" | custom-call | tf_op jit(solution)/shard_map/column_sums/pallas_call | solution.py:150
  139.3 12.2 %all_to_all.48.part_ref = f32[16,16,128]{2,1,0:T(8,128)} all-to-all(f32[16,16,128]{2,1,0:T(8,128)} %column_sums.4), channel_id=1, replica_groups=mesh['row'=16,'col'=8] {'row'}, dimensions={0} | all-to-all | bytes 262144 | tf_op jit(solution)/shard_map/all_to_all | solution.py:278
  151.5 6.7 %row_sums.4 = f32[8,8,128]{2,1,0:T(8,128)} custom-call(f32[16,16,128]{2,1,0:T(8,128)} %all_to_all.48.part_ref, f32[2048,1024]{1,0:T(8,128)} %get-tuple-element.19.kt_ref.refs_4_), custom_call_target="tpu_custom_call" | custom-call | tf_op jit(solution)/shard_map/row_sums/pallas_call | solution.py:162
  158.2 9.4 %all_to_all.49.part_ref.refs_1_ = f32[8,8,128]{2,1,0:T(8,128)} all-to-all(f32[8,8,128]{2,1,0:T(8,128)} %row_sums.4), channel_id=1, replica_groups=mesh['row'=16,'col'=8] {'col'}, dimensions={0} | all-to-all | bytes 65536 | tf_op jit(solution)/shard_map/all_to_all | solution.py:278
  167.6 6.8 %column_sums.5 = f32[16,16,128]{2,1,0:T(8,128)} custom-call(f32[8,8,128]{2,1,0:T(8,128)} %all_to_all.49.part_ref.refs_1_, f32[2048,1024]{1,0:T(8,128)} %get-tuple-element.19.kt_ref.refs_4_), custom_call_target="tpu_custom_call" | custom-call | tf_op jit(solution)/shard_map/column_sums/pallas_call | solution.py:150
  174.4 12.2 %all_to_all.50.part_ref.refs_2_ = f32[16,16,128]{2,1,0:T(8,128)} all-to-all(f32[16,16,128]{2,1,0:T(8,128)} %column_sums.5), channel_id=1, replica_groups=mesh['row'=16,'col'=8] {'row'}, dimensions={0} | all-to-all | bytes 262144 | tf_op jit(solution)/shard_map/all_to_all | solution.py:278
  186.5 6.7 %row_sums.5 = f32[8,8,128]{2,1,0:T(8,128)} custom-call(f32[16,16,128]{2,1,0:T(8,128)} %all_to_all.50.part_ref.refs_2_, f32[2048,1024]{1,0:T(8,128)} %get-tuple-element.19.kt_ref.refs_4_), custom_call_target="tpu_custom_call" | custom-call | tf_op jit(solution)/shard_map/row_sums/pallas_call | solution.py:162
  193.2 9.4 %all_to_all.51.refs_3_ = f32[8,8,128]{2,1,0:T(8,128)} all-to-all(f32[8,8,128]{2,1,0:T(8,128)} %row_sums.5), channel_id=1, replica_groups=mesh['row'=16,'col'=8] {'col'}, dimensions={0} | all-to-all | bytes 65536 | tf_op jit(solution)/shard_map/all_to_all | solution.py:278
  202.6 28.8 %unit_grads.1 = (f32[2048,768]{1,0:T(8,128)}, f32[1024,768]{1,0:T(8,128)}, f32[8,128]{1,0:T(8,128)}) custom-call(f32[8,8,128]{2,1,0:T(8,128)} %all_to_all.45.part_ref.refs_0_, f32[8,8,128]{2,1,0:T(8,128)} %all_to_all.49.part_ref.refs_1_, f32[16,16,128]{2,1,0:T(8,128)} %all_to_all.50.part_ref.refs_2_, f32[8,8,128]{2,1,0:T(8,128)} %all_to_all.51.refs_3_, ...), custom_call_target="tpu_custom_call" | custom-call | tf_op jit(solution)/shard_map/unit_grads/pallas_call | solution.py:210
  243.9 5.6 %collective-permute-done.24 = f32[128,768]{1,0:T(8,128)S(1)} collective-permute-done((f32[128,768]{1,0:T(8,128)}, f32[128,768]{1,0:T(8,128)S(1)}, u32[]{:S(2)}, u32[]{:S(2)}) %collective-permute-start.24) | collective-permute-done | bytes 393248 | tf_op jit(solution)/shard_map/ppermute | solution.py:241
  264.4 5.3 %all-to-all-done.7 = f32[8,8,128]{2,1,0:T(8,128)S(1)} async-done(((f32[8,8,128]{2,1,0:T(8,128)}), f32[8,8,128]{2,1,0:T(8,128)S(1)}, u32[]{:S(2)}, u32[]{:S(2)}) %all-to-all-start.7) | async-done | bytes 32800 | tf_op jit(solution)/shard_map/all_to_all | solution.py:278
  270.3 6.0 %all-to-all-start.8 = ((f32[16,8,128]{2,1,0:T(8,128)}), f32[16,8,128]{2,1,0:T(8,128)S(1)}, u32[]{:S(2)}, u32[]{:S(2)}) async-start(f32[16,8,128]{2,1,0:T(8,128)} %broadcast_in_dim.5), calls=%async_computation.8 | async-start | bytes 131072 | tf_op jit(solution)/shard_map/all_to_all | solution.py:278
  276.5 7.5 %all-to-all-done.8 = f32[16,8,128]{2,1,0:T(8,128)S(1)} async-done(((f32[16,8,128]{2,1,0:T(8,128)}), f32[16,8,128]{2,1,0:T(8,128)S(1)}, u32[]{:S(2)}, u32[]{:S(2)}) %all-to-all-start.8) | async-done | bytes 65568 | tf_op jit(solution)/shard_map/all_to_all | solution.py:278
  304.4 3.8 %collective-permute-done.21 = f32[64,768]{1,0:T(8,128)S(1)} collective-permute-done((f32[64,768]{1,0:T(8,128)S(1)}, f32[64,768]{1,0:T(8,128)S(1)}, u32[]{:S(2)}, u32[]{:S(2)}) %collective-permute-start.21) | collective-permute-done | bytes 196640 | tf_op jit(solution)/shard_map/ppermute | solution.py:241
  (140 shorter events, 83.9 us)
Async XLA Ops:
  7.2 59.1 %all-gather.2.cloned.1.call-start = ((), (), s32[]{:S(2)}) async-start(), calls=%async_computation.10 | async-start | bytes 3538944 | tf_op jit(solution)/shard_map/all_gather | solution.py:287
  9.4 299.8 %reduce-scatter.2.cloned.1.call-start = ((), (), s32[]{:S(2)}) async-start(), calls=%async_computation.11 | async-start | bytes 3538944 | tf_op jit(solution)/shard_map/reduce_scatter | solution.py:301
  17.9 16.0 %collective-permute-start.11 = (f32[32,768]{1,0:T(8,128)S(1)}, f32[32,768]{1,0:T(8,128)S(1)}, u32[]{:S(2)}, u32[]{:S(2)}) collective-permute-start(f32[32,768]{1,0:T(8,128)S(1)} %slice.157), channel_id=1, source_target_pairs={{0,96},{8,104},{16,112},{24,120},{32,0},{40,8},{48,16},{56,24},{64... | collective-permute-start | bytes 294920 | tf_op jit(solution)/shard_map/ppermute | solution.py:237
  21.6 12.2 %collective-permute-start.10 = (f32[32,768]{1,0:T(8,128)S(1)}, f32[32,768]{1,0:T(8,128)S(1)}, u32[]{:S(2)}, u32[]{:S(2)}) collective-permute-start(f32[32,768]{1,0:T(8,128)S(1)} %slice.156), channel_id=1, source_target_pairs={{0,32},{8,40},{16,48},{24,56},{32,64},{40,72},{48,80},{56,88},{64,... | collective-permute-start | bytes 294920 | tf_op jit(solution)/shard_map/ppermute | solution.py:237
  21.7 8.8 %collective-permute-start.3 = (f32[32,768]{1,0:T(8,128)S(1)}, f32[32,768]{1,0:T(8,128)S(1)}, u32[]{:S(2)}, u32[]{:S(2)}) collective-permute-start(f32[32,768]{1,0:T(8,128)S(1)} %slice.153), channel_id=1, source_target_pairs={{0,24},{8,0},{16,8},{24,16},{32,56},{40,32},{48,40},{56,48},{64,88... | collective-permute-start | bytes 294920 | tf_op jit(solution)/shard_map/ppermute | solution.py:241
  30.5 17.6 %collective-permute-start.5 = (f32[256,768]{1,0:T(8,128)S(1)}, f32[256,768]{1,0:T(8,128)S(1)}, u32[]{:S(2)}, u32[]{:S(2)}) collective-permute-start(f32[256,768]{1,0:T(8,128)S(1)} %constant_dynamic-update-slice_fusion.refs_0_), channel_id=1, source_target_pairs={{0,96},{8,104},{16,112},{24,120},{32,0},{40,8},{48,16},{56,24},{64... | collective-permute-start | bytes 2359304 | tf_op jit(solution)/shard_map/ppermute | solution.py:237
  33.8 18.1 %collective-permute-start.4 = (f32[256,768]{1,0:T(8,128)S(1)}, f32[256,768]{1,0:T(8,128)S(1)}, u32[]{:S(2)}, u32[]{:S(2)}) collective-permute-start(f32[256,768]{1,0:T(8,128)S(1)} %constant_dynamic-update-slice_fusion.refs_0_), channel_id=1, source_target_pairs={{0,32},{8,40},{16,48},{24,56},{32,64},{40,72},{48,80},{56,88},{64,... | collective-permute-start | bytes 2359304 | tf_op jit(solution)/shard_map/ppermute | solution.py:237
  33.9 18.9 %collective-permute-start.13 = (f32[256,768]{1,0:T(8,128)S(1)}, f32[256,768]{1,0:T(8,128)S(1)}, u32[]{:S(2)}, u32[]{:S(2)}) collective-permute-start(f32[256,768]{1,0:T(8,128)S(1)} %constant_dynamic-update-slice_fusion.5.refs_4_), channel_id=1, source_target_pairs={{0,24},{8,0},{16,8},{24,16},{32,56},{40,32},{48,40},{56,48},{64,88... | collective-permute-start | bytes 2359304 | tf_op jit(solution)/shard_map/ppermute | solution.py:241
  33.9 19.7 %collective-permute-start.12 = (f32[256,768]{1,0:T(8,128)S(1)}, f32[256,768]{1,0:T(8,128)S(1)}, u32[]{:S(2)}, u32[]{:S(2)}) collective-permute-start(f32[256,768]{1,0:T(8,128)S(1)} %constant_dynamic-update-slice_fusion.5.refs_4_), channel_id=1, source_target_pairs={{0,8},{8,16},{16,24},{24,0},{32,40},{40,48},{48,56},{56,32},{64,72... | collective-permute-start | bytes 2359304 | tf_op jit(solution)/shard_map/ppermute | solution.py:241
  48.2 9.1 %collective-permute-start.7 = (f32[128,768]{1,0:T(8,128)S(1)}, f32[128,768]{1,0:T(8,128)}, u32[]{:S(2)}, u32[]{:S(2)}) collective-permute-start(f32[128,768]{1,0:T(8,128)S(1)} %slice.155), channel_id=1, source_target_pairs={{0,96},{8,104},{16,112},{24,120},{32,0},{40,8},{48,16},{56,24},{64... | collective-permute-start | bytes 1179656 | tf_op jit(solution)/shard_map/ppermute | solution.py:237
  52.8 9.3 %collective-permute-start.6 = (f32[128,768]{1,0:T(8,128)}, f32[128,768]{1,0:T(8,128)}, u32[]{:S(2)}, u32[]{:S(2)}) collective-permute-start(f32[128,768]{1,0:T(8,128)} %slice.154), channel_id=1, source_target_pairs={{0,32},{8,40},{16,48},{24,56},{32,64},{40,72},{48,80},{56,88},{64,... | collective-permute-start | bytes 1179656 | tf_op jit(solution)/shard_map/ppermute | solution.py:237
  53.6 10.5 %collective-permute-start.15 = (f32[128,768]{1,0:T(8,128)}, f32[128,768]{1,0:T(8,128)}, u32[]{:S(2)}, u32[]{:S(2)}) collective-permute-start(f32[128,768]{1,0:T(8,128)} %slice.159), channel_id=1, source_target_pairs={{0,24},{8,0},{16,8},{24,16},{32,56},{40,32},{48,40},{56,48},{64,88... | collective-permute-start | bytes 1179656 | tf_op jit(solution)/shard_map/ppermute | solution.py:241
  54.5 9.7 %collective-permute-start.14 = (f32[128,768]{1,0:T(8,128)}, f32[128,768]{1,0:T(8,128)}, u32[]{:S(2)}, u32[]{:S(2)}) collective-permute-start(f32[128,768]{1,0:T(8,128)} %slice.158), channel_id=1, source_target_pairs={{0,8},{8,16},{16,24},{24,0},{32,40},{40,48},{48,56},{56,32},{64,72... | collective-permute-start | bytes 1179656 | tf_op jit(solution)/shard_map/ppermute | solution.py:241
  237.3 12.2 %collective-permute-start.24 = (f32[128,768]{1,0:T(8,128)}, f32[128,768]{1,0:T(8,128)S(1)}, u32[]{:S(2)}, u32[]{:S(2)}) collective-permute-start(f32[128,768]{1,0:T(8,128)} %get-tuple-element.41), channel_id=1, source_target_pairs={{0,8},{8,16},{16,24},{24,0},{32,40},{40,48},{48,56},{56,32},{64,72... | collective-permute-start | bytes 1179656 | tf_op jit(solution)/shard_map/ppermute | solution.py:241
  237.9 11.7 %collective-permute-start.26 = (f32[128,768]{1,0:T(8,128)}, f32[128,768]{1,0:T(8,128)}, u32[]{:S(2)}, u32[]{:S(2)}) collective-permute-start(f32[128,768]{1,0:T(8,128)} %get-tuple-element.42), channel_id=1, source_target_pairs={{0,24},{8,0},{16,8},{24,16},{32,56},{40,32},{48,40},{56,48},{64,88... | collective-permute-start | bytes 1179656 | tf_op jit(solution)/shard_map/ppermute | solution.py:241
  240.6 15.6 %collective-permute-start.16 = (f32[128,768]{1,0:T(8,128)S(1)}, f32[128,768]{1,0:T(8,128)S(1)}, u32[]{:S(2)}, u32[]{:S(2)}) collective-permute-start(f32[128,768]{1,0:T(8,128)S(1)} %get-tuple-element.35), channel_id=1, source_target_pairs={{0,32},{8,40},{16,48},{24,56},{32,64},{40,72},{48,80},{56,88},{64,... | collective-permute-start | bytes 1179656 | tf_op jit(solution)/shard_map/ppermute | solution.py:237
  240.9 15.3 %collective-permute-start.18 = (f32[128,768]{1,0:T(8,128)S(1)}, f32[128,768]{1,0:T(8,128)S(1)}, u32[]{:S(2)}, u32[]{:S(2)}) collective-permute-start(f32[128,768]{1,0:T(8,128)S(1)} %get-tuple-element.36), channel_id=1, source_target_pairs={{0,96},{8,104},{16,112},{24,120},{32,0},{40,8},{48,16},{56,24},{64... | collective-permute-start | bytes 1179656 | tf_op jit(solution)/shard_map/ppermute | solution.py:237
  252.1 33.1 %collective-permute-start.27 = (f32[256,768]{1,0:T(8,128)}, f32[256,768]{1,0:T(8,128)}, u32[]{:S(2)}, u32[]{:S(2)}) collective-permute-start(f32[256,768]{1,0:T(8,128)} %pad_maximum_fusion.5), channel_id=1, source_target_pairs={{0,24},{8,0},{16,8},{24,16},{32,56},{40,32},{48,40},{56,48},{64,88... | collective-permute-start | bytes 2359304 | tf_op jit(solution)/shard_map/ppermute | solution.py:241
  256.2 29.1 %collective-permute-start.25 = (f32[256,768]{1,0:T(8,128)}, f32[256,768]{1,0:T(8,128)}, u32[]{:S(2)}, u32[]{:S(2)}) collective-permute-start(f32[256,768]{1,0:T(8,128)} %pad_maximum_fusion.4), channel_id=1, source_target_pairs={{0,8},{8,16},{16,24},{24,0},{32,40},{40,48},{48,56},{56,32},{64,72... | collective-permute-start | bytes 2359304 | tf_op jit(solution)/shard_map/ppermute | solution.py:241
  257.3 33.1 %collective-permute-start.19 = (f32[256,768]{1,0:T(8,128)}, f32[256,768]{1,0:T(8,128)}, u32[]{:S(2)}, u32[]{:S(2)}) collective-permute-start(f32[256,768]{1,0:T(8,128)} %pad_maximum_fusion.3), channel_id=1, source_target_pairs={{0,96},{8,104},{16,112},{24,120},{32,0},{40,8},{48,16},{56,24},{64... | collective-permute-start | bytes 2359304 | tf_op jit(solution)/shard_map/ppermute | solution.py:237
  259.1 31.3 %collective-permute-start.17 = (f32[256,768]{1,0:T(8,128)}, f32[256,768]{1,0:T(8,128)}, u32[]{:S(2)}, u32[]{:S(2)}) collective-permute-start(f32[256,768]{1,0:T(8,128)} %pad_maximum_fusion.2), channel_id=1, source_target_pairs={{0,32},{8,40},{16,48},{24,56},{32,64},{40,72},{48,80},{56,88},{64,... | collective-permute-start | bytes 2359304 | tf_op jit(solution)/shard_map/ppermute | solution.py:237
  261.0 8.7 %all-to-all-start.7 = ((f32[8,8,128]{2,1,0:T(8,128)}), f32[8,8,128]{2,1,0:T(8,128)S(1)}, u32[]{:S(2)}, u32[]{:S(2)}) async-start(f32[8,8,128]{2,1,0:T(8,128)} %broadcast_in_dim.4), calls=%async_computation.7 | async-start | bytes 65536 | tf_op jit(solution)/shard_map/all_to_all | solution.py:278
  270.3 13.7 %all-to-all-start.8 = ((f32[16,8,128]{2,1,0:T(8,128)}), f32[16,8,128]{2,1,0:T(8,128)S(1)}, u32[]{:S(2)}, u32[]{:S(2)}) async-start(f32[16,8,128]{2,1,0:T(8,128)} %broadcast_in_dim.5), calls=%async_computation.8 | async-start | bytes 131072 | tf_op jit(solution)/shard_map/all_to_all | solution.py:278
  287.1 8.2 %collective-permute-start.28 = (f32[32,768]{1,0:T(8,128)S(1)}, f32[32,768]{1,0:T(8,128)S(1)}, u32[]{:S(2)}, u32[]{:S(2)}) collective-permute-start(f32[32,768]{1,0:T(8,128)S(1)} %get-tuple-element.53), channel_id=1, source_target_pairs={{0,32},{8,40},{16,48},{24,56},{32,64},{40,72},{48,80},{56,88},{64,... | collective-permute-start | bytes 294920 | tf_op jit(solution)/shard_map/ppermute | solution.py:237
  (24 other events, 261.2 us)
Sparse Core Ops, SparseCore 0:
  10.3 30.4 all-gather.1
  231.5 32.1 reduce-scatter.1

commit v2 on v0

v2 whole, which is shorter than its diff:
```python
import jax
import jax.numpy as jnp
from jax import lax
from jax.experimental import pallas as pl
from jax.experimental.pallas import tpu as pltpu
from jax.sharding import PartitionSpec as P

ITERS = 3
F32 = jnp.float32
BF16 = jnp.bfloat16
MIB = 1024 * 1024
NEAR = (0, -1, 1, 2)


def vmem():
    return pl.BlockSpec(memory_space=pltpu.VMEM)


def smem():
    return pl.BlockSpec(memory_space=pltpu.SMEM)


def f32(*shape):
    return jax.ShapeDtypeStruct(shape, F32)


def bf16(*shape):
    return jax.ShapeDtypeStruct(shape, BF16)


def call(kernel, name, outs, *args, pos=None, scratch=(), mib=7, flops=0):
    specs = [vmem()] * len(args)
    if pos is not None:
        specs, args = [smem()] + specs, (pos,) + args
    size = lambda arrays: sum(a.size * a.dtype.itemsize for a in arrays)
    return pl.pallas_call(
        kernel,
        out_shape=list(outs),
        in_specs=specs,
        out_specs=[vmem()] * len(outs),
        scratch_shapes=list(scratch),
        compiler_params=pltpu.CompilerParams(vmem_limit_bytes=mib * MIB),
        cost_estimate=pl.CostEstimate(
            flops=flops, bytes_accessed=size(args) + size(outs), transcendentals=0
        ),
        name=name,
    )(*args)


def split(value):
    high = value.astype(BF16)
    return high, (value - high.astype(F32)).astype(BF16)


def dot3(lhs, rhs, dims):
    (lh, ll), (rh, rl) = lhs, rhs
    dot = lambda p, q: lax.dot_general(p, q, (dims, ((), ())), preferred_element_type=F32)
    return dot(lh, rh) + (dot(lh, rl) + dot(ll, rh))


def inverse_length(x):
    return lax.rsqrt(jnp.sum(x * x, axis=1, keepdims=True) + 1e-06)


def unit_kernel(a_ref, v_ref, au_ref, vt_ref, vb_ref):
    a = a_ref[...]
    au_ref[...] = a * inverse_length(a)
    v = v_ref[...]
    v = v * inverse_length(v)
    vt_ref[...] = v[:64]
    vb_ref[...] = v[64:]


LAYOUT = (
    ((0, 0), (1, 0)),
    ((0, 1), (0, 2), (1, 1), (1, 2)),
    ((0, 3), (1, 3)),
)


def join_kernel(half, pos_ref, own, left, right, far, out_ref):
    for j, ref in enumerate((own, left, right, far)):
        at = ((pos_ref[1 - half] + NEAR[j] + 4) % 4) * 64
        out_ref[pl.ds(pl.multiple_of(at, 64), 64), :] = ref[...]


def halves_kernel(left, right, a_ref, b_ref):
    a_ref[...] = left[0:128, :]
    b_ref[...] = right[128:256, :]


def pieces_body(total, pieces, ah_ref, al_ref, k_ref, vh_ref, vl_ref):
    at = 0
    for piece in pieces:
        rows = slice(at, at + piece.shape[0])
        vh_ref[rows, :], vl_ref[rows, :] = split(piece[...])
        at += piece.shape[0]
        if at % 256 == 0:
            rows = slice(at - 256, at)
            video = (vh_ref[rows, :], vl_ref[rows, :])
            k = jnp.exp(20.0 * dot3(video, (ah_ref[...], al_ref[...]), ((1,), (1,))))
            k_ref[rows, :] = k
            total = total + jnp.sum(k.reshape(-1, 8, k.shape[1]), axis=0)
    return total


def scores_own_kernel(a_ref, p_ref, q_ref, ah_ref, al_ref, k_ref, vh_ref, vl_ref, sum_ref):
    ah_ref[...], al_ref[...] = split(a_ref[...])
    sum_ref[...] = pieces_body(0.0, (p_ref, q_ref), ah_ref, al_ref, k_ref, vh_ref, vl_ref)


def scores_near_kernel(ah_ref, al_ref, in_ref, p0, p1, p2, p3, k_ref, vh_ref, vl_ref, sum_ref):
    sum_ref[...] = pieces_body(in_ref[...], (p0, p1, p2, p3), ah_ref, al_ref, k_ref, vh_ref, vl_ref)


def scores_far_kernel(ah_ref, al_ref, in_ref, p0, p1, q0, q1, k_ref, vh_ref, vl_ref, sum_ref):
    total = pieces_body(in_ref[...], (p0, p1, q0, q1), ah_ref, al_ref, k_ref, vh_ref, vl_ref)
    put_lanes(sum_ref, jnp.sum(total, axis=0, keepdims=True))


def put_lanes(ref, row):
    for m in range(8):
        part = row[:, m * 128 : m * 128 + 128]
        for d in range(8):
            ref[d, m : m + 1, :] = part


def scale_of(part_ref):
    return 1.0 / jnp.sum(part_ref[...], axis=0)


def chunk_of(pos_ref, half, j, b):
    return half * 8 + ((pos_ref[half] + NEAR[j] + 4) % 4) * 2 + b


def chunks(pos_ref, k_refs):
    for ref, blocks in zip(k_refs, LAYOUT):
        for n, (half, j) in enumerate(blocks):
            for b in range(2):
                yield ref, n * 256 + b * 128, chunk_of(pos_ref, half, j, b)


def down(scale_ref, chunk):
    return jnp.broadcast_to(scale_ref[pl.ds(chunk, 1), :], (128, 128)).T


def columns_kernel(pos_ref, part_ref, k1_ref, k2_ref, k3_ref, out_ref):
    r = scale_of(part_ref)
    for ref, at, chunk in chunks(pos_ref, (k1_ref, k2_ref, k3_ref)):
        acc = ref[at : at + 128, 0:128] * r[0:1, :]
        for m in range(1, 8):
            acc = acc + ref[at : at + 128, m * 128 : m * 128 + 128] * r[m : m + 1, :]
        row = jnp.sum(acc.T, axis=0, keepdims=True)
        for d in range(16):
            out_ref[d, pl.ds(chunk, 1), :] = row


def fold(value):
    return jnp.sum(value.reshape(16, 8, 128), axis=0)


def rows_kernel(pos_ref, part_ref, k1_ref, k2_ref, k3_ref, out_ref, scale_ref):
    scale_ref[...] = scale_of(part_ref)
    acc = [0.0] * 8
    for ref, at, chunk in chunks(pos_ref, (k1_ref, k2_ref, k3_ref)):
        c = down(scale_ref, chunk)
        for m in range(8):
            acc[m] = acc[m] + fold(ref[at : at + 128, m * 128 : m * 128 + 128] * c)
    put_lanes(out_ref, jnp.concatenate([jnp.sum(a, axis=0, keepdims=True) for a in acc], axis=1))


def last_rows_kernel(pos_ref, part_ref, rpart_ref, tot_ref, k1_ref, k2_ref, k3_ref, out_ref, scale_ref):
    scale_ref[...] = scale_of(part_ref)
    acc, weighted = [0.0] * 8, [0.0] * 8
    for ref, at, chunk in chunks(pos_ref, (k1_ref, k2_ref, k3_ref)):
        c = down(scale_ref, chunk)
        for m in range(8):
            kernel = ref[at : at + 128, m * 128 : m * 128 + 128]
            prod = kernel * c
            acc[m] = acc[m] + fold(prod)
            weighted[m] = weighted[m] + fold(prod * jnp.log(kernel))
    r = scale_of(rpart_ref)
    logs = jnp.log(jnp.sum(tot_ref[...], axis=0))
    terms = sum(r[m : m + 1] * (weighted[m] - logs[m : m + 1] * acc[m]) for m in range(8))
    put_lanes(out_ref, jnp.concatenate([jnp.sum(a, axis=0, keepdims=True) for a in acc], axis=1))
    for d in range(8):
        out_ref[d, 8:16, :] = terms


def grad_scales(count, tot_ref, rp_ref, cp_ref, tp_ref, c_ref, r_ref, w_ref):
    c_ref[...] = scale_of(cp_ref)
    r = scale_of(rp_ref) * (20.0 / count)
    w = r * jnp.sum(tp_ref[:, 0:8, :], axis=0) / jnp.sum(tot_ref[...], axis=0)
    for m in range(8):
        lanes = slice(m * 128, m * 128 + 128)
        r_ref[:, lanes] = jnp.broadcast_to(r[m : m + 1], (8, 128))
        w_ref[:, lanes] = jnp.broadcast_to(w[m : m + 1], (8, 128))


def grad_block(pos_ref, half, j, k_ref, at, c_ref, r_ref, w_ref):
    c = jnp.concatenate([down(c_ref, chunk_of(pos_ref, half, j, b)) for b in range(2)], axis=0)
    c = jnp.concatenate([c] * 8, axis=1)
    return split(k_ref[at : at + 256, :] * (w_ref[0:1, :] - r_ref[0:1, :] * c))


SCALES = [pltpu.VMEM((16, 128), F32), pltpu.VMEM((8, 1024), F32), pltpu.VMEM((8, 1024), F32)]


def far_kernel(count, pos_ref, tot_ref, rp_ref, cp_ref, tp_ref, k_ref, ah_ref, al_ref,
               yu_ref, yd_ref, xu_ref, xd_ref, c_ref, r_ref, w_ref):
    grad_scales(count, tot_ref, rp_ref, cp_ref, tp_ref, c_ref, r_ref, w_ref)
    for half, (u_ref, d_ref) in enumerate(((yu_ref, yd_ref), (xu_ref, xd_ref))):
        g = grad_block(pos_ref, half, 3, k_ref, half * 256, c_ref, r_ref, w_ref)
        out = dot3(g, (ah_ref[...], al_ref[...]), ((1,), (0,)))
        u_ref[0:128, :] = out[:128]
        d_ref[0:128, :] = out[128:]
    terms = jnp.concatenate([jnp.sum(tp_ref[:, 8:16, :], axis=0)] * 6, axis=1)
    yu_ref[128:136, :] = terms
    yd_ref[128:136, :] = terms


def audio_body(pos_ref, layouts, start, u_ref, c_ref, r_ref, w_ref):
    for k_ref, h_ref, l_ref, blocks in layouts:
        for n, (half, j) in enumerate(blocks):
            at = slice(n * 256, n * 256 + 256)
            g = grad_block(pos_ref, half, j, k_ref, n * 256, c_ref, r_ref, w_ref)
            for m in range(4):
                lanes = slice(m * 256, m * 256 + 256)
                part = tuple(v[:, lanes] for v in g)
                out = dot3(part, (h_ref[at, :], l_ref[at, :]), ((0,), (0,)))
                u_ref[lanes, :] = out if start is None else start[lanes, :] + out
            start = u_ref


def audio_first_kernel(count, pos_ref, tot_ref, rp_ref, cp_ref, tp_ref, k1_ref, k3_ref,
                       h1_ref, l1_ref, h3_ref, l3_ref, u_ref, c_ref, r_ref, w_ref):
    grad_scales(count, tot_ref, rp_ref, cp_ref, tp_ref, c_ref, r_ref, w_ref)
    layouts = ((k1_ref, h1_ref, l1_ref, LAYOUT[0]), (k3_ref, h3_ref, l3_ref, LAYOUT[2]))
    audio_body(pos_ref, layouts, None, u_ref, c_ref, r_ref, w_ref)


def audio_second_kernel(count, pos_ref, tot_ref, rp_ref, cp_ref, tp_ref, k2_ref, h2_ref, l2_ref,
                        in_ref, u_ref, c_ref, r_ref, w_ref):
    grad_scales(count, tot_ref, rp_ref, cp_ref, tp_ref, c_ref, r_ref, w_ref)
    audio_body(pos_ref, ((k2_ref, h2_ref, l2_ref, LAYOUT[1]),), in_ref, u_ref, c_ref, r_ref, w_ref)


def near_kernel(count, pos_ref, tot_ref, rp_ref, cp_ref, tp_ref, k_ref, ah_ref, al_ref,
                yl_ref, yr_ref, xl_ref, xr_ref, yu_ref, yd_ref, xu_ref, xd_ref, c_ref, r_ref, w_ref):
    grad_scales(count, tot_ref, rp_ref, cp_ref, tp_ref, c_ref, r_ref, w_ref)
    for n, (ref, left, right) in enumerate((
        (yd_ref, None, yr_ref), (yu_ref, yl_ref, None), (xd_ref, None, xr_ref), (xu_ref, xl_ref, None)
    )):
        half, j = LAYOUT[1][n]
        g = grad_block(pos_ref, half, j, k_ref, n * 256, c_ref, r_ref, w_ref)
        out = dot3(g, (ah_ref[...], al_ref[...]), ((1,), (0,)))
        ref[0:128, :] = out[:128] if left is None else out[:128] + left[0:128, :]
        ref[128:256, :] = out[128:] if right is None else out[128:] + right[0:128, :]
    yu_ref[256:264, :] = yl_ref[128:136, :]


def own_kernel(count, pos_ref, tot_ref, rp_ref, cp_ref, tp_ref, k_ref, ah_ref, al_ref,
               y_ref, x_ref, c_ref, r_ref, w_ref):
    grad_scales(count, tot_ref, rp_ref, cp_ref, tp_ref, c_ref, r_ref, w_ref)
    for half, ref in enumerate((y_ref, x_ref)):
        g = grad_block(pos_ref, half, 0, k_ref, half * 256, c_ref, r_ref, w_ref)
        ref[...] = dot3(g, (ah_ref[...], al_ref[...]), ((1,), (0,)))


def ordered_sum(me, values, order_ref):
    for k, value in enumerate(values):
        order_ref[pl.ds(pl.multiple_of(((me + k) % 4) * 8, 8), 8), :] = value
    return jnp.sum(order_ref[...].reshape(4, 8, 128), axis=0)


def middle_kernel(pos_ref, tp_ref, yl_ref, yr_ref, y_ref, x_ref, yu_ref, yd_ref, xu_ref, xd_ref,
                  y1_ref, y2_ref, y3_ref, y0_ref, x1_ref, x2_ref, x3_ref, x0_ref, sum_ref, order_ref):
    terms = ordered_sum(
        pos_ref[0],
        (jnp.sum(tp_ref[:, 8:16, :], axis=0), yr_ref[128:136, 0:128], yu_ref[256:264, 0:128],
         yl_ref[128:136, 0:128]),
        order_ref,
    )
    for half, (own, up, down, outs) in enumerate((
        (y_ref, yu_ref, yd_ref, (y0_ref, y1_ref, y2_ref, y3_ref)),
        (x_ref, xu_ref, xd_ref, (x0_ref, x1_ref, x2_ref, x3_ref)),
    )):
        sum_ref[...] = own[...] + up[0:256, :] + down[...]
        for k, ref in enumerate(outs):
            at = ((pos_ref[1 - half] + k) % 4) * 64
            ref[0:64, :] = sum_ref[pl.ds(pl.multiple_of(at, 64), 64), :]
            if half == 0:
                ref[64:72, :] = jnp.concatenate([terms] * 6, axis=1)


def project(x, grad):
    inv = inverse_length(x)
    unit = x * inv
    return (grad - unit * jnp.sum(unit * grad, axis=1, keepdims=True)) * inv


def video_kernel(count, pos_ref, v_ref, y0, y1, y2, y3, x0, x1, x2, x3, out_ref, loss_ref, order_ref):
    top = y0[0:64, :] + y1[0:64, :] + y2[0:64, :] + y3[0:64, :]
    bottom = x0[...] + x1[...] + x2[...] + x3[...]
    out_ref[0:64, :] = project(v_ref[0:64, :], top)
    out_ref[64:128, :] = project(v_ref[64:128, :], bottom)
    terms = ordered_sum(
        pos_ref[1], tuple(ref[64:72, 0:128] for ref in (y0, y3, y2, y1)), order_ref
    )
    loss_ref[...] = jnp.full((1, 1), -jnp.sum(terms) / count)


def audio_project_kernel(x_ref, grad_ref, out_ref):
    out_ref[...] = project(x_ref[...], grad_ref[...])


def step_y(v, k):
    return lax.ppermute(v, "row", [(i, ((i // 4 + k) % 4) * 4 + i % 4) for i in range(16)])


def step_x(v, k):
    return lax.ppermute(v, "row", [(i, (i // 4) * 4 + (i % 4 + k) % 4) for i in range(16)])


def swap(part, axis):
    return lax.all_to_all(part, axis, 0, 0, tiled=True)


def local(audio, video):
    count = audio.shape[0] * 128
    bind = lambda kernel: lambda *refs: kernel(count, *refs)
    row = lax.axis_index("row")
    pos = jnp.stack([row // 4, row % 4]).astype(jnp.int32)
    audio_unit, vt, vb = call(
        unit_kernel, "unit_rows", [f32(128, 768), f32(64, 768), f32(64, 768)], audio, video
    )
    audio_tile = lax.all_gather(audio_unit, "col", axis=0, tiled=True)
    join = lambda half, *parts: call(
        lambda *refs: join_kernel(half, *refs), "join", [f32(256, 768)], *parts, pos=pos, mib=4
    )[0]
    xl, xr, yl, yr = step_x(vt, 1), step_x(vt, -1), step_y(vb, 1), step_y(vb, -1)
    first = join(0, vt, xl, xr, step_x(vt, 2))
    second = join(1, vb, yl, yr, step_y(yr, -1))
    fl, fr, sl, sr = step_y(first, 1), step_y(first, -1), step_x(second, 1), step_x(second, -1)
    flops = 3 * 2 * 1024 * 768
    ah, al, k1, h1, l1, sums = call(
        scores_own_kernel, "scores_own",
        [bf16(1024, 768), bf16(1024, 768), f32(512, 1024), bf16(512, 768), bf16(512, 768), f32(8, 1024)],
        audio_tile, first, second, flops=512 * flops,
    )
    fl, fr, sl, sr, sums = lax.optimization_barrier((fl, fr, sl, sr, sums))
    halves = lambda left, right: call(halves_kernel, "halves", [f32(128, 768)] * 2, left, right, mib=4)
    a, b = halves(fl, fr)
    c, d = halves(sl, sr)
    far = (step_y(a, 1), step_y(b, -1), step_x(c, 1), step_x(d, -1))
    k2, h2, l2, sums = call(
        scores_near_kernel, "scores_near",
        [f32(1024, 1024), bf16(1024, 768), bf16(1024, 768), f32(8, 1024)],
        ah, al, sums, fl, fr, sl, sr, flops=1024 * flops,
    )
    k3, h3, l3, part = call(
        scores_far_kernel, "scores_far",
        [f32(512, 1024), bf16(512, 768), bf16(512, 768), f32(8, 8, 128)],
        ah, al, sums, *far, flops=512 * flops,
    )
    ks = (k1, k2, k3)
    scale = pltpu.VMEM((16, 128), F32)
    totals = swap(part, "col")
    rpart = totals
    for step in range(ITERS):
        cpart = swap(call(columns_kernel, "column_sums", [f32(16, 16, 128)], rpart, *ks, pos=pos, mib=9)[0], "row")
        if step < ITERS - 1:
            part = call(rows_kernel, "row_sums", [f32(8, 8, 128)], cpart, *ks, pos=pos, mib=9, scratch=[scale])[0]
            rpart = swap(part, "col")
    part = call(last_rows_kernel, "row_sums_and_loss", [f32(8, 16, 128)], cpart, rpart, totals, *ks,
                pos=pos, mib=9, scratch=[scale])[0]
    tpart = swap(part, "col")

    vectors = (totals, rpart, cpart, tpart)
    block = f32(256, 768)
    yu, yd, xu, xd = call(
        bind(far_kernel), "video_far", [f32(136, 768), f32(136, 768), f32(128, 768), f32(128, 768)],
        *vectors, k3, ah, al, pos=pos, scratch=SCALES, flops=512 * flops,
    )
    after, yu = lax.optimization_barrier((tpart, yu))
    yl, yr, xl, xr = step_y(yu, 1), step_y(yd, -1), step_x(xu, 1), step_x(xd, -1)
    (half_audio,) = call(
        bind(audio_first_kernel), "audio_first", [f32(1024, 768)], totals, rpart, cpart, after, k1, k3,
        h1, l1, h3, l3, pos=pos, scratch=SCALES, flops=1024 * flops,
    )
    yl, yr, xl, xr, half_audio = lax.optimization_barrier((yl, yr, xl, xr, half_audio))
    yu, yd, xu, xd = call(
        bind(near_kernel), "video_near", [f32(264, 768), block, block, block],
        *vectors, k2, ah, al, yl, yr, xl, xr, pos=pos, scratch=SCALES, flops=1024 * flops,
    )
    yu, yd, xu, xd, half_audio = lax.optimization_barrier((yu, yd, xu, xd, half_audio))
    yu, yd, xu, xd = step_y(yu, 1), step_y(yd, -1), step_x(xu, 1), step_x(xd, -1)
    (full_audio,) = call(
        bind(audio_second_kernel), "audio_second", [f32(1024, 768)], *vectors, k2, h2, l2, half_audio,
        pos=pos, scratch=SCALES, flops=1024 * flops,
    )
    unit_audio = lax.psum_scatter(full_audio, "col", scatter_dimension=0, tiled=True)
    after, full_audio = lax.optimization_barrier((tpart, full_audio))
    y_own, x_own = call(
        bind(own_kernel), "video_own", [block, block], totals, rpart, cpart, after, k1, ah, al, pos=pos,
        scratch=SCALES, flops=512 * flops,
    )
    yu, yd, xu, xd, y_own = lax.optimization_barrier((yu, yd, xu, xd, y_own))
    order = pltpu.VMEM((32, 128), F32)
    y1, y2, y3, y0, x1, x2, x3, x0 = call(
        middle_kernel, "video_middle", [f32(72, 768)] * 4 + [f32(64, 768)] * 4,
        tpart, yl, yr, y_own, x_own, yu, yd, xu, xd, pos=pos, scratch=[pltpu.VMEM((256, 768), F32), order],
    )
    y1, y2, y3 = step_x(y1, 1), step_x(y2, 2), step_x(y3, 3)
    x1, x2, x3 = step_y(x1, 1), step_y(x2, 2), step_y(x3, 3)
    (audio_grad,) = call(audio_project_kernel, "audio_grad", [f32(128, 768)], audio, unit_audio)
    video_grad, loss = call(
        bind(video_kernel), "video_grad", [f32(128, 768), f32(1, 1)],
        video, y0, y1, y2, y3, x0, x1, x2, x3, pos=pos, scratch=[order],
    )
    return (loss[0, 0], audio_grad, video_grad)


def solution(mesh):
    in_specs = (P(("row", "col"), None), P(("col", "row"), None))
    out_specs = (P(), P(("row", "col"), None), P(("col", "row"), None))
    return jax.shard_map(local, mesh=mesh, in_specs=in_specs, out_specs=out_specs, check_vma=False)
```

time: 562 us -> 243 us (0.43); the launches traced: 552 us -> 243 us
  waiting for transfers between devices: 185 us -> 33.8 us
  blocking collectives: 229 us -> 79.8 us
  matrix products: 80.2 us -> 0 us
  Pallas kernels: 0 us -> 56.4 us
  starting transfers between devices: 0.38 us -> 45.1 us
  other arithmetic: 42.2 us -> 0.07 us
  local copies, waits for them, and re-layouts: 0.01 us -> 13 us
    psum x8 -> x0, blocking collectives: 229 us -> none  [the longest x3 113 us: local(): col_sums = lax.psum(jnp.sum(kernel * row_scale[:, None], axis=0), 'row')]
    psum x2 -> x0, waiting for transfers between devices: 93.4 us -> none  [the longest x1 93.3 us: local(): lax.psum(20.0 * jnp.dot(score_grad.T, audio_tile, precision=HIGH, preferr...]
    dot_general x3 -> x0, matrix products: 80.2 us -> none  [the longest x1 27.7 us: local(): jnp.dot(score_grad.T, audio_tile, precision=HIGH, preferred_element_type=...]
    all_to_all x0 -> x7, blocking collectives: none -> 79.8 us  [swap(): return lax.all_to_all(part, axis, 0, 0, tiled=True)]
    all_gather x1 -> x0, waiting for transfers between devices: 63.8 us -> none  [local(): video_tile = lax.all_gather(video_unit, 'row', axis=0, tiled=True)]
    pallas_call x0 -> x22, Pallas kernels: none -> 56.4 us  [call(): pl.pallas_call(kernel, out_shape=list(outs), in_specs=specs, out_specs=[v...]
    ppermute x0 -> x28, starting transfers between devices: none -> 45 us  [the longest x14 23.7 us: step_x(): lax.ppermute(v, 'row', [(i, i // 4 * 4 + (i % 4 + k) % 4) for i in range(...]
    reduce_sum x10 -> x0, other arithmetic: 34.7 us -> none  [the longest x3 13.6 us: local(): col_sums = lax.psum(jnp.sum(kernel * row_scale[:, None], axis=0), 'row')]
  transfers between devices with their start and end apart: 4 -> 30, of which waited for: 3 -> 11; matrix products, arithmetic and copies ran while one was open for 6% -> 0% of each run, Pallas kernels for 0% -> 11%
where the time goes in v2:
time: 243 us
  blocking collectives  79.8 us (33%)
  Pallas kernels  56.4 us (23%)
  starting transfers between devices  45.1 us (19%)
  waiting for transfers between devices  33.8 us (14%)
  between operations  14.6 us (6%)
  local copies, waits for them, and re-layouts  13 us (5%)
    all_to_all x7, blocking collectives, swap(): return lax.all_to_all(part, axis, 0, 0, tiled=True)  79.8 us
    pallas_call x22, Pallas kernels, call(): pl.pallas_call(kernel, out_shape=list(outs), in_specs=specs, out_specs=[v...  56.4 us
    ppermute x14, starting transfers between devices, step_x(): lax.ppermute(v, 'row', [(i, i // 4 * 4 + (i % 4 + k) % 4) for i in range(...  23.7 us
    ppermute x14, starting transfers between devices, step_y(): lax.ppermute(v, 'row', [(i, (i // 4 + k) % 4 * 4 + i % 4) for i in range(...  21.3 us
    ppermute x14, waiting for transfers between devices, step_x(): lax.ppermute(v, 'row', [(i, i // 4 * 4 + (i % 4 + k) % 4) for i in range(...  14.3 us
    ppermute x14, waiting for transfers between devices, step_y(): lax.ppermute(v, 'row', [(i, (i // 4 + k) % 4 * 4 + i % 4) for i in range(...  14.3 us
    unnamed x30, local copies, waits for them, and re-layouts  13 us
    all_gather x1, waiting for transfers between devices, local(): audio_tile = lax.all_gather(audio_unit, 'col', axis=0, tiled=True)  5.17 us
  transfers between devices with their start and end apart: 30, of which 11 were waited for; matrix products, arithmetic and copies ran while one was open for 0% of the time, Pallas kernels for 11%

profile of v2, /device:TPU:0, one launch (start us, length us, event | category | flops | bytes accessed | tf_op | source)
XLA Modules:
  0.0 242.7 jit_solution(12482873644036825970)
XLA Ops:
  18.4 3.2 %collective-permute-start.5 = (f32[64,768]{1,0:T(8,128)S(1)}, f32[64,768]{1,0:T(8,128)S(1)}, u32[]{:S(2)}, u32[]{:S(2)}) collective-permute-start(f32[64,768]{1,0:T(8,128)S(1)} %collective-permute-done.4.refs_3_), channel_id=1, source_target_pairs={{0,96},{8,104},{16,112},{24,120},{32,0},{40,8},{48,16},{56,24},{64... | collective-permute-start | bytes 589832 | tf_op jit(solution)/shard_map/ppermute | solution.py:318
  27.6 3.2 %collective-permute-start.7 = (f32[256,768]{1,0:T(8,128)}, f32[256,768]{1,0:T(8,128)}, u32[]{:S(2)}, u32[]{:S(2)}) collective-permute-start(f32[256,768]{1,0:T(8,128)} %join.2.p_ref), channel_id=1, source_target_pairs={{0,96},{8,104},{16,112},{24,120},{32,0},{40,8},{48,16},{56,24},{64... | collective-permute-start | bytes 2359304 | tf_op jit(solution)/shard_map/ppermute | solution.py:318
  35.6 5.2 %all-gather.2.cloned.1.call-done.a_ref = f32[1024,768]{1,0:T(8,128)} async-done(((f32[128,768]{1,0:T(8,128)}), f32[1024,768]{1,0:T(8,128)}) %all-gather.2.cloned.1.call-update) | async-done | bytes 3145744 | tf_op jit(solution)/shard_map/all_gather | solution.py:337
  42.6 4.1 %scores_own.1 = (bf16[1024,768]{1,0:T(8,128)(2,1)S(1)}, bf16[1024,768]{1,0:T(8,128)(2,1)S(1)}, f32[512,1024]{1,0:T(8,128)S(1)}, bf16[512,768]{1,0:T(8,128)(2,1)S...) custom-call(f32[1024,768]{1,0:T(8,128)S(1)} %copy-done.6, f32[256,768]{1,0:T(8,128)} %join.2.p_ref, ...), custom_call_target="tpu_custom_call" | custom-call | flops 2415919104 | bytes 11567104 | tf_op jit(solution)/shard_map/scores_own/pallas_call | solution.py:36
  47.1 4.3 %collective-permute-done.8.p2.left = f32[256,768]{1,0:T(8,128)} collective-permute-done((f32[256,768]{1,0:T(8,128)}, f32[256,768]{1,0:T(8,128)}, u32[]{:S(2)}, u32[]{:S(2)}) %collective-permute-start.8) | collective-permute-done | bytes 786464 | tf_op jit(solution)/shard_map/ppermute | solution.py:322
  57.4 3.6 %collective-permute-start.13 = (f32[128,768]{1,0:T(8,128)S(1)}, f32[128,768]{1,0:T(8,128)S(1)}, u32[]{:S(2)}, u32[]{:S(2)}) collective-permute-start(f32[128,768]{1,0:T(8,128)S(1)} %get-tuple-element.82), channel_id=1, source_target_pairs={{0,24},{8,0},{16,8},{24,16},{32,56},{40,32},{48,40},{56,48},{64,88... | collective-permute-start | bytes 1179656 | tf_op jit(solution)/shard_map/ppermute | solution.py:322
  61.0 6.8 %scores_near.1 = (f32[1024,1024]{1,0:T(8,128)S(1)}, bf16[1024,768]{1,0:T(8,128)(2,1)S(1)}, bf16[1024,768]{1,0:T(8,128)(2,1)S(1)}, f32[8,1024]{1,0:T(8,128)S(1)}) custom-call(bf16[1024,768]{1,0:T(8,128)(2,1)S(1)} %get-tuple-element.70.ah_ref.refs_6_, bf16[1024,768]{1,0:T(8,128)(2,1)S(1)} %get-tuple-element.71.al_ref.refs_7_, ...), custom_call_target="tpu_custom_call" | custom-call | flops 4831838208 | bytes 13697024 | tf_op jit(solution)/shard_map/scores_near/pallas_call | solution.py:36
  70.5 10.6 %all_to_all.35.part_ref.tot_ref.refs_1_ = f32[8,8,128]{2,1,0:T(8,128)S(1)} all-to-all(f32[8,8,128]{2,1,0:T(8,128)S(1)} %get-tuple-element.83), channel_id=1, replica_groups=mesh['row'=16,'col'=8] {'col'}, dimensions={0} | all-to-all | bytes 65536 | tf_op jit(solution)/shard_map/all_to_all | solution.py:326
  82.2 11.4 %all_to_all.36.part_ref = f32[16,16,128]{2,1,0:T(8,128)S(1)} all-to-all(f32[16,16,128]{2,1,0:T(8,128)S(1)} %column_sums.3), channel_id=1, replica_groups=mesh['row'=16,'col'=8] {'row'}, dimensions={0} | all-to-all | bytes 262144 | tf_op jit(solution)/shard_map/all_to_all | solution.py:326
  94.8 7.8 %all_to_all.37.part_ref = f32[8,8,128]{2,1,0:T(8,128)S(1)} all-to-all(f32[8,8,128]{2,1,0:T(8,128)S(1)} %row_sums.2), channel_id=1, replica_groups=mesh['row'=16,'col'=8] {'col'}, dimensions={0} | all-to-all | bytes 65536 | tf_op jit(solution)/shard_map/all_to_all | solution.py:326
  103.8 11.1 %all_to_all.38.part_ref = f32[16,16,128]{2,1,0:T(8,128)S(1)} all-to-all(f32[16,16,128]{2,1,0:T(8,128)S(1)} %column_sums.4), channel_id=1, replica_groups=mesh['row'=16,'col'=8] {'row'}, dimensions={0} | all-to-all | bytes 262144 | tf_op jit(solution)/shard_map/all_to_all | solution.py:326
  116.1 7.8 %all_to_all.39.part_ref.rpart_ref.refs_2_ = f32[8,8,128]{2,1,0:T(8,128)S(1)} all-to-all(f32[8,8,128]{2,1,0:T(8,128)S(1)} %row_sums.3), channel_id=1, replica_groups=mesh['row'=16,'col'=8] {'col'}, dimensions={0} | all-to-all | bytes 65536 | tf_op jit(solution)/shard_map/all_to_all | solution.py:326
  125.1 23.2 %all_to_all.40.part_ref.refs_3_ = f32[16,16,128]{2,1,0:T(8,128)S(1)} all-to-all(f32[16,16,128]{2,1,0:T(8,128)S(1)} %column_sums.5), channel_id=1, replica_groups=mesh['row'=16,'col'=8] {'row'}, dimensions={0} | all-to-all | bytes 262144 | tf_op jit(solution)/shard_map/all_to_all | solution.py:326
  150.6 8.0 %all_to_all.41.refs_4_.tp_ref = f32[8,16,128]{2,1,0:T(8,128)S(1)} all-to-all(f32[8,16,128]{2,1,0:T(8,128)S(1)} %row_sums_and_loss.1), channel_id=1, replica_groups=mesh['row'=16,'col'=8] {'col'}, dimensions={0} | all-to-all | bytes 131072 | tf_op jit(solution)/shard_map/all_to_all | solution.py:326
  158.6 3.4 %video_far.1 = (f32[136,768]{1,0:T(8,128)S(1)}, f32[136,768]{1,0:T(8,128)S(1)}, f32[128,768]{1,0:T(8,128)S(1)}, f32[128,768]{1,0:T(8,128)S(1)}) custom-call(s32[2]{0:T(128)S(1)} %pad_add_fusion.refs_0_.pos_ref, f32[8,8,128]{2,1,0:T(8,128)S(1)} %all_to_all.35.part_ref.tot_ref.refs_1_, f32[8,8,128]{2,1,0:T(8,128)S(1)} %all_to_all.39.part_ref.rpart_ref.refs_2_, ...), custom_call_target="tpu_custom_call" | custom-call | flops 2415919104 | bytes 7127048 | tf_op jit(solution)/shard_map/video_far/pallas_call | solution.py:36
  168.5 5.9 %audio_first.1.refs_8_ = f32[1024,768]{1,0:T(8,128)S(1)} custom-call(s32[2]{0:T(128)S(1)} %pad_add_fusion.refs_0_.pos_ref, f32[8,8,128]{2,1,0:T(8,128)S(1)} %all_to_all.35.part_ref.tot_ref.refs_1_, f32[8,8,128]{2,1,0:T(8,128)S(1)} %all_to_all.39.part_ref.rpart_ref.refs_2_, f32[16,16,128]{2,1,0:T(8,128)S(1)} %all_to_all.40.part_ref.refs_3_, ...), custom_call_target="tpu_custom_call" | custom-call | flops 4831838208 | bytes 10747912 | tf_op jit(solution)/shard_map/audio_first/pallas_call | solution.py:36
  176.7 5.9 %video_near.1 = (f32[264,768]{1,0:T(8,128)S(1)}, f32[256,768]{1,0:T(8,128)S(1)}, f32[256,768]{1,0:T(8,128)S(1)}, f32[256,768]{1,0:T(8,128)S(1)}) custom-call(s32[2]{0:T(128)S(1)} %pad_add_fusion.refs_0_.pos_ref, f32[8,8,128]{2,1,0:T(8,128)S(1)} %all_to_all.35.part_ref.tot_ref.refs_1_, f32[8,8,128]{2,1,0:T(8,128)S(1)} %all_to_all.39.part_ref.rpart_ref.refs_2_, ...), custom_call_target="tpu_custom_call" | custom-call | flops 4831838208 | bytes 12394504 | tf_op jit(solution)/shard_map/video_near/pallas_call | solution.py:36
  186.2 6.0 %audio_second.1 = f32[1024,768]{1,0:T(8,128)S(1)} custom-call(s32[2]{0:T(128)S(1)} %pad_add_fusion.refs_0_.pos_ref, f32[8,8,128]{2,1,0:T(8,128)S(1)} %all_to_all.35.part_ref.tot_ref.refs_1_, f32[8,8,128]{2,1,0:T(8,128)S(1)} %all_to_all.39.part_ref.rpart_ref.refs_2_, f32[16,16,128]{2,1,0:T(8,128)S(1)} %all_to_all.40.part_ref.refs_3_, ...), custom_call_target="tpu_custom_call" | custom-call | flops 4831838208 | bytes 13893640 | tf_op jit(solution)/shard_map/audio_second/pallas_call | solution.py:36
  197.2 3.2 %collective-permute-start.21 = (f32[256,768]{1,0:T(8,128)}, f32[256,768]{1,0:T(8,128)S(1)}, u32[]{:S(2)}, u32[]{:S(2)}) collective-permute-start(f32[256,768]{1,0:T(8,128)} %copy-done.8), channel_id=1, source_target_pairs={{0,24},{8,0},{16,8},{24,16},{32,56},{40,32},{48,40},{56,48},{64,88... | collective-permute-start | bytes 2359304 | tf_op jit(solution)/shard_map/ppermute | solution.py:322
  203.3 3.5 %video_own.1 = (f32[256,768]{1,0:T(8,128)S(1)}, f32[256,768]{1,0:T(8,128)S(1)}) custom-call(s32[2]{0:T(128)S(1)} %pad_add_fusion.refs_0_.pos_ref, f32[8,8,128]{2,1,0:T(8,128)S(1)} %all_to_all.35.part_ref.tot_ref.refs_1_, f32[8,8,128]{2,1,0:T(8,128)S(1)} %all_to_all.39.part_ref.rpart_ref.refs_2_, f32[16,16,128]{2,1,0:T(8,128)S(1)} %all_to_all.40.part_ref.refs_3_, ...), custom_call_target="tpu_custom_call" | custom-call | flops 2415919104 | bytes 7077896 | tf_op jit(solution)/shard_map/video_own/pallas_call | solution.py:36
  206.8 5.7 %collective-permute-done.19.yd_ref = f32[256,768]{1,0:T(8,128)S(1)} collective-permute-done((f32[256,768]{1,0:T(8,128)}, f32[256,768]{1,0:T(8,128)S(1)}, u32[]{:S(2)}, u32[]{:S(2)}) %collective-permute-start.19) | collective-permute-done | bytes 786464 | tf_op jit(solution)/shard_map/ppermute | solution.py:318
  212.5 3.3 %collective-permute-done.20.xu_ref = f32[256,768]{1,0:T(8,128)S(1)} collective-permute-done((f32[256,768]{1,0:T(8,128)}, f32[256,768]{1,0:T(8,128)S(1)}, u32[]{:S(2)}, u32[]{:S(2)}) %collective-permute-start.20) | collective-permute-done | bytes 786464 | tf_op jit(solution)/shard_map/ppermute | solution.py:322
  217.8 3.6 %collective-permute-start.23 = (f32[72,768]{1,0:T(8,128)S(1)}, f32[72,768]{1,0:T(8,128)S(1)}, u32[]{:S(2)}, u32[]{:S(2)}) collective-permute-start(f32[72,768]{1,0:T(8,128)S(1)} %get-tuple-element.123), channel_id=1, source_target_pairs={{0,16},{8,24},{16,0},{24,8},{32,48},{40,56},{48,32},{56,40},{64,80... | collective-permute-start | bytes 663560 | tf_op jit(solution)/shard_map/ppermute | solution.py:322
  225.9 3.5 %collective-permute-done.26.refs_8_ = f32[64,768]{1,0:T(8,128)S(1)} collective-permute-done((f32[64,768]{1,0:T(8,128)S(1)}, f32[64,768]{1,0:T(8,128)S(1)}, u32[]{:S(2)}, u32[]{:S(2)}) %collective-permute-start.26) | collective-permute-done | bytes 196640 | tf_op jit(solution)/shard_map/ppermute | solution.py:318
  (98 shorter events, 74.0 us)
Async XLA Ops:
  7.2 33.6 %all-gather.2.cloned.1.call-start = ((), (), s32[]{:S(2)}) async-start(), calls=%async_computation.8 | async-start | bytes 3538944 | tf_op jit(solution)/shard_map/all_gather | solution.py:337
  10.1 223.6 %reduce-scatter.2.cloned.1.call-start = ((), (), s32[]{:S(2)}) async-start(), calls=%async_computation.9 | async-start | bytes 3538944 | tf_op jit(solution)/shard_map/reduce_scatter | solution.py:402
  14.8 9.6 %collective-permute-start.1 = (f32[64,768]{1,0:T(8,128)S(1)}, f32[64,768]{1,0:T(8,128)S(1)}, u32[]{:S(2)}, u32[]{:S(2)}) collective-permute-start(f32[64,768]{1,0:T(8,128)S(1)} %get-tuple-element.68.refs_1_), channel_id=1, source_target_pairs={{0,24},{8,0},{16,8},{24,16},{32,56},{40,32},{48,40},{56,48},{64,88... | collective-permute-start | bytes 589832 | tf_op jit(solution)/shard_map/ppermute | solution.py:322
  18.4 12.5 %collective-permute-start.3 = (f32[64,768]{1,0:T(8,128)S(1)}, f32[64,768]{1,0:T(8,128)S(1)}, u32[]{:S(2)}, u32[]{:S(2)}) collective-permute-start(f32[64,768]{1,0:T(8,128)S(1)} %get-tuple-element.69.refs_1_), channel_id=1, source_target_pairs={{0,32},{8,40},{16,48},{24,56},{32,64},{40,72},{48,80},{56,88},{64,... | collective-permute-start | bytes 589832 | tf_op jit(solution)/shard_map/ppermute | solution.py:318
  18.4 12.5 %collective-permute-start.5 = (f32[64,768]{1,0:T(8,128)S(1)}, f32[64,768]{1,0:T(8,128)S(1)}, u32[]{:S(2)}, u32[]{:S(2)}) collective-permute-start(f32[64,768]{1,0:T(8,128)S(1)} %collective-permute-done.4.refs_3_), channel_id=1, source_target_pairs={{0,96},{8,104},{16,112},{24,120},{32,0},{40,8},{48,16},{56,24},{64... | collective-permute-start | bytes 589832 | tf_op jit(solution)/shard_map/ppermute | solution.py:318
  27.6 19.5 %collective-permute-start.6 = (f32[256,768]{1,0:T(8,128)}, f32[256,768]{1,0:T(8,128)S(1)}, u32[]{:S(2)}, u32[]{:S(2)}) collective-permute-start(f32[256,768]{1,0:T(8,128)} %join.2.p_ref), channel_id=1, source_target_pairs={{0,32},{8,40},{16,48},{24,56},{32,64},{40,72},{48,80},{56,88},{64,... | collective-permute-start | bytes 2359304 | tf_op jit(solution)/shard_map/ppermute | solution.py:318
  27.6 19.5 %collective-permute-start.7 = (f32[256,768]{1,0:T(8,128)}, f32[256,768]{1,0:T(8,128)}, u32[]{:S(2)}, u32[]{:S(2)}) collective-permute-start(f32[256,768]{1,0:T(8,128)} %join.2.p_ref), channel_id=1, source_target_pairs={{0,96},{8,104},{16,112},{24,120},{32,0},{40,8},{48,16},{56,24},{64... | collective-permute-start | bytes 2359304 | tf_op jit(solution)/shard_map/ppermute | solution.py:318
  32.3 19.1 %collective-permute-start.8 = (f32[256,768]{1,0:T(8,128)}, f32[256,768]{1,0:T(8,128)}, u32[]{:S(2)}, u32[]{:S(2)}) collective-permute-start(f32[256,768]{1,0:T(8,128)} %join.3.q_ref), channel_id=1, source_target_pairs={{0,8},{8,16},{16,24},{24,0},{32,40},{40,48},{48,56},{56,32},{64,72... | collective-permute-start | bytes 2359304 | tf_op jit(solution)/shard_map/ppermute | solution.py:322
  33.5 17.9 %collective-permute-start.9 = (f32[256,768]{1,0:T(8,128)}, f32[256,768]{1,0:T(8,128)}, u32[]{:S(2)}, u32[]{:S(2)}) collective-permute-start(f32[256,768]{1,0:T(8,128)} %join.3.q_ref), channel_id=1, source_target_pairs={{0,24},{8,0},{16,8},{24,16},{32,56},{40,32},{48,40},{56,48},{64,88... | collective-permute-start | bytes 2359304 | tf_op jit(solution)/shard_map/ppermute | solution.py:322
  52.6 15.2 %collective-permute-start.10 = (f32[128,768]{1,0:T(8,128)S(1)}, f32[128,768]{1,0:T(8,128)S(1)}, u32[]{:S(2)}, u32[]{:S(2)}) collective-permute-start(f32[128,768]{1,0:T(8,128)S(1)} %get-tuple-element.79), channel_id=1, source_target_pairs={{0,32},{8,40},{16,48},{24,56},{32,64},{40,72},{48,80},{56,88},{64,... | collective-permute-start | bytes 1179656 | tf_op jit(solution)/shard_map/ppermute | solution.py:318
  52.7 15.1 %collective-permute-start.11 = (f32[128,768]{1,0:T(8,128)S(1)}, f32[128,768]{1,0:T(8,128)S(1)}, u32[]{:S(2)}, u32[]{:S(2)}) collective-permute-start(f32[128,768]{1,0:T(8,128)S(1)} %get-tuple-element.80), channel_id=1, source_target_pairs={{0,96},{8,104},{16,112},{24,120},{32,0},{40,8},{48,16},{56,24},{64... | collective-permute-start | bytes 1179656 | tf_op jit(solution)/shard_map/ppermute | solution.py:318
  57.3 10.4 %collective-permute-start.12 = (f32[128,768]{1,0:T(8,128)S(1)}, f32[128,768]{1,0:T(8,128)S(1)}, u32[]{:S(2)}, u32[]{:S(2)}) collective-permute-start(f32[128,768]{1,0:T(8,128)S(1)} %get-tuple-element.81), channel_id=1, source_target_pairs={{0,8},{8,16},{16,24},{24,0},{32,40},{40,48},{48,56},{56,32},{64,72... | collective-permute-start | bytes 1179656 | tf_op jit(solution)/shard_map/ppermute | solution.py:322
  57.4 10.4 %collective-permute-start.13 = (f32[128,768]{1,0:T(8,128)S(1)}, f32[128,768]{1,0:T(8,128)S(1)}, u32[]{:S(2)}, u32[]{:S(2)}) collective-permute-start(f32[128,768]{1,0:T(8,128)S(1)} %get-tuple-element.82), channel_id=1, source_target_pairs={{0,24},{8,0},{16,8},{24,16},{32,56},{40,32},{48,40},{56,48},{64,88... | collective-permute-start | bytes 1179656 | tf_op jit(solution)/shard_map/ppermute | solution.py:322
  161.9 14.7 %collective-permute-start.14 = (f32[136,768]{1,0:T(8,128)S(1)}, f32[136,768]{1,0:T(8,128)S(1)}, u32[]{:S(2)}, u32[]{:S(2)}) collective-permute-start(f32[136,768]{1,0:T(8,128)S(1)} %get-tuple-element.88), channel_id=1, source_target_pairs={{0,32},{8,40},{16,48},{24,56},{32,64},{40,72},{48,80},{56,88},{64,... | collective-permute-start | bytes 1253384 | tf_op jit(solution)/shard_map/ppermute | solution.py:318
  162.2 14.4 %collective-permute-start.15 = (f32[136,768]{1,0:T(8,128)S(1)}, f32[136,768]{1,0:T(8,128)S(1)}, u32[]{:S(2)}, u32[]{:S(2)}) collective-permute-start(f32[136,768]{1,0:T(8,128)S(1)} %get-tuple-element.89), channel_id=1, source_target_pairs={{0,96},{8,104},{16,112},{24,120},{32,0},{40,8},{48,16},{56,24},{64... | collective-permute-start | bytes 1253384 | tf_op jit(solution)/shard_map/ppermute | solution.py:318
  165.2 11.4 %collective-permute-start.16 = (f32[128,768]{1,0:T(8,128)S(1)}, f32[128,768]{1,0:T(8,128)S(1)}, u32[]{:S(2)}, u32[]{:S(2)}) collective-permute-start(f32[128,768]{1,0:T(8,128)S(1)} %get-tuple-element.90), channel_id=1, source_target_pairs={{0,8},{8,16},{16,24},{24,0},{32,40},{40,48},{48,56},{56,32},{64,72... | collective-permute-start | bytes 1179656 | tf_op jit(solution)/shard_map/ppermute | solution.py:322
  165.8 10.8 %collective-permute-start.17 = (f32[128,768]{1,0:T(8,128)S(1)}, f32[128,768]{1,0:T(8,128)S(1)}, u32[]{:S(2)}, u32[]{:S(2)}) collective-permute-start(f32[128,768]{1,0:T(8,128)S(1)} %get-tuple-element.91), channel_id=1, source_target_pairs={{0,24},{8,0},{16,8},{24,16},{32,56},{40,32},{48,40},{56,48},{64,88... | collective-permute-start | bytes 1179656 | tf_op jit(solution)/shard_map/ppermute | solution.py:322
  193.9 21.9 %collective-permute-start.18 = (f32[264,768]{1,0:T(8,128)}, f32[264,768]{1,0:T(8,128)S(1)}, u32[]{:S(2)}, u32[]{:S(2)}) collective-permute-start(f32[264,768]{1,0:T(8,128)} %copy-done.7), channel_id=1, source_target_pairs={{0,32},{8,40},{16,48},{24,56},{32,64},{40,72},{48,80},{56,88},{64,... | collective-permute-start | bytes 2433032 | tf_op jit(solution)/shard_map/ppermute | solution.py:318
  194.0 18.5 %collective-permute-start.19 = (f32[256,768]{1,0:T(8,128)}, f32[256,768]{1,0:T(8,128)S(1)}, u32[]{:S(2)}, u32[]{:S(2)}) collective-permute-start(f32[256,768]{1,0:T(8,128)} %copy-done.10), channel_id=1, source_target_pairs={{0,96},{8,104},{16,112},{24,120},{32,0},{40,8},{48,16},{56,24},{64... | collective-permute-start | bytes 2359304 | tf_op jit(solution)/shard_map/ppermute | solution.py:318
  197.2 18.6 %collective-permute-start.20 = (f32[256,768]{1,0:T(8,128)}, f32[256,768]{1,0:T(8,128)S(1)}, u32[]{:S(2)}, u32[]{:S(2)}) collective-permute-start(f32[256,768]{1,0:T(8,128)} %copy-done.9), channel_id=1, source_target_pairs={{0,8},{8,16},{16,24},{24,0},{32,40},{40,48},{48,56},{56,32},{64,72... | collective-permute-start | bytes 2359304 | tf_op jit(solution)/shard_map/ppermute | solution.py:322
  197.2 18.6 %collective-permute-start.21 = (f32[256,768]{1,0:T(8,128)}, f32[256,768]{1,0:T(8,128)S(1)}, u32[]{:S(2)}, u32[]{:S(2)}) collective-permute-start(f32[256,768]{1,0:T(8,128)} %copy-done.8), channel_id=1, source_target_pairs={{0,24},{8,0},{16,8},{24,16},{32,56},{40,32},{48,40},{56,48},{64,88... | collective-permute-start | bytes 2359304 | tf_op jit(solution)/shard_map/ppermute | solution.py:322
  216.9 15.1 %collective-permute-start.22 = (f32[72,768]{1,0:T(8,128)S(1)}, f32[72,768]{1,0:T(8,128)S(1)}, u32[]{:S(2)}, u32[]{:S(2)}) collective-permute-start(f32[72,768]{1,0:T(8,128)S(1)} %get-tuple-element.122), channel_id=1, source_target_pairs={{0,8},{8,16},{16,24},{24,0},{32,40},{40,48},{48,56},{56,32},{64,72... | collective-permute-start | bytes 663560 | tf_op jit(solution)/shard_map/ppermute | solution.py:322
  217.8 14.2 %collective-permute-start.23 = (f32[72,768]{1,0:T(8,128)S(1)}, f32[72,768]{1,0:T(8,128)S(1)}, u32[]{:S(2)}, u32[]{:S(2)}) collective-permute-start(f32[72,768]{1,0:T(8,128)S(1)} %get-tuple-element.123), channel_id=1, source_target_pairs={{0,16},{8,24},{16,0},{24,8},{32,48},{40,56},{48,32},{56,40},{64,80... | collective-permute-start | bytes 663560 | tf_op jit(solution)/shard_map/ppermute | solution.py:322
  221.4 10.7 %collective-permute-start.24 = (f32[72,768]{1,0:T(8,128)S(1)}, f32[72,768]{1,0:T(8,128)S(1)}, u32[]{:S(2)}, u32[]{:S(2)}) collective-permute-start(f32[72,768]{1,0:T(8,128)S(1)} %get-tuple-element.124), channel_id=1, source_target_pairs={{0,24},{8,0},{16,8},{24,16},{32,56},{40,32},{48,40},{56,48},{64,88... | collective-permute-start | bytes 663560 | tf_op jit(solution)/shard_map/ppermute | solution.py:322
  (21 other events, 354.5 us)
Sparse Core Ops, SparseCore 0:
  10.3 30.4 all-gather.1
  194.0 33.4 reduce-scatter.1

commit v3 on v2

--- a/solution.py
+++ b/solution.py
@@ -1,3 +1,5 @@
+import math
+
 import jax
 import jax.numpy as jnp
 from jax import lax
@@ -28,17 +30,19 @@
     return jax.ShapeDtypeStruct(shape, BF16)
 
 
-def call(kernel, name, outs, *args, pos=None, scratch=(), mib=7, flops=0):
+def call(kernel, name, outs, *args, pos=None, scratch=(), mib=7, flops=0, aliases=None, far_out=False):
     specs = [vmem()] * len(args)
     if pos is not None:
         specs, args = [smem()] + specs, (pos,) + args
-    size = lambda arrays: sum(a.size * a.dtype.itemsize for a in arrays)
+    size = lambda arrays: sum(math.prod(a.shape) * a.dtype.itemsize for a in arrays)
+    hbm = pl.BlockSpec(memory_space=pltpu.HBM)
     return pl.pallas_call(
         kernel,
-        out_shape=list(outs),
+        out_shape=[pltpu.HBM(o.shape, o.dtype) if far_out else o for o in outs],
         in_specs=specs,
-        out_specs=[vmem()] * len(outs),
+        out_specs=[hbm if far_out else vmem()] * len(outs),
         scratch_shapes=list(scratch),
+        input_output_aliases=aliases or {},
         compiler_params=pltpu.CompilerParams(vmem_limit_bytes=mib * MIB),
         cost_estimate=pl.CostEstimate(
             flops=flops, bytes_accessed=size(args) + size(outs), transcendentals=0
@@ -78,10 +82,14 @@
 )
 
 
-def join_kernel(half, pos_ref, own, left, right, far, out_ref):
+def join_kernel(half, pos_ref, own, left, right, far, out_ref, sems):
+    copies = []
     for j, ref in enumerate((own, left, right, far)):
-        at = ((pos_ref[1 - half] + NEAR[j] + 4) % 4) * 64
-        out_ref[pl.ds(pl.multiple_of(at, 64), 64), :] = ref[...]
+        at = pl.multiple_of(((pos_ref[1 - half] + NEAR[j] + 4) % 4) * 64, 64)
+        copies.append(pltpu.make_async_copy(ref, out_ref.at[pl.ds(at, 64), :], sems.at[j]))
+        copies[j].start()
+    for copy in copies:
+        copy.wait()
 
 
 def halves_kernel(left, right, a_ref, b_ref):
@@ -219,9 +227,9 @@
     yd_ref[128:136, :] = terms
 
 
-def audio_body(pos_ref, layouts, start, u_ref, c_ref, r_ref, w_ref):
-    for k_ref, h_ref, l_ref, blocks in layouts:
-        for n, (half, j) in enumerate(blocks):
+def audio_body(pos_ref, layouts, start, u_ref, c_ref, r_ref, w_ref, copies=None):
+    for k_ref, h_ref, l_ref, first, blocks in layouts:
+        for n, (half, j) in enumerate(blocks, first):
             at = slice(n * 256, n * 256 + 256)
             g = grad_block(pos_ref, half, j, k_ref, n * 256, c_ref, r_ref, w_ref)
             for m in range(4):
@@ -229,34 +237,56 @@
                 part = tuple(v[:, lanes] for v in g)
                 out = dot3(part, (h_ref[at, :], l_ref[at, :]), ((0,), (0,)))
                 u_ref[lanes, :] = out if start is None else start[lanes, :] + out
+                if copies is not None and n == first + len(blocks) - 1:
+                    copies[m].start()
             start = u_ref
 
 
-def audio_first_kernel(count, pos_ref, tot_ref, rp_ref, cp_ref, tp_ref, k1_ref, k3_ref,
-                       h1_ref, l1_ref, h3_ref, l3_ref, u_ref, c_ref, r_ref, w_ref):
+def audio_first_kernel(count, pos_ref, tot_ref, rp_ref, cp_ref, tp_ref, k1_ref, k2_ref, k3_ref,
+                       h1_ref, l1_ref, h2_ref, l2_ref, h3_ref, l3_ref, u_ref, c_ref, r_ref, w_ref):
     grad_scales(count, tot_ref, rp_ref, cp_ref, tp_ref, c_ref, r_ref, w_ref)
-    layouts = ((k1_ref, h1_ref, l1_ref, LAYOUT[0]), (k3_ref, h3_ref, l3_ref, LAYOUT[2]))
+    layouts = (
+        (k1_ref, h1_ref, l1_ref, 0, LAYOUT[0]),
+        (k3_ref, h3_ref, l3_ref, 0, LAYOUT[2]),
+        (k2_ref, h2_ref, l2_ref, 0, LAYOUT[1][:2]),
+    )
     audio_body(pos_ref, layouts, None, u_ref, c_ref, r_ref, w_ref)
 
 
 def audio_second_kernel(count, pos_ref, tot_ref, rp_ref, cp_ref, tp_ref, k2_ref, h2_ref, l2_ref,
-                        in_ref, u_ref, c_ref, r_ref, w_ref):
+                        in_ref, u_ref, c_ref, r_ref, w_ref, sum_ref, sems):
     grad_scales(count, tot_ref, rp_ref, cp_ref, tp_ref, c_ref, r_ref, w_ref)
-    audio_body(pos_ref, ((k2_ref, h2_ref, l2_ref, LAYOUT[1]),), in_ref, u_ref, c_ref, r_ref, w_ref)
+    copies = [
+        pltpu.make_async_copy(
+            sum_ref.at[pl.ds(m * 256, 256), :], u_ref.at[pl.ds(m * 256, 256), :], sems.at[m]
+        )
+        for m in range(4)
+    ]
+    layouts = ((k2_ref, h2_ref, l2_ref, 2, LAYOUT[1][2:]),)
+    audio_body(pos_ref, layouts, in_ref, sum_ref, c_ref, r_ref, w_ref, copies)
+    for copy in copies:
+        copy.wait()
 
 
 def near_kernel(count, pos_ref, tot_ref, rp_ref, cp_ref, tp_ref, k_ref, ah_ref, al_ref,
-                yl_ref, yr_ref, xl_ref, xr_ref, yu_ref, yd_ref, xu_ref, xd_ref, c_ref, r_ref, w_ref):
+                yl_ref, yr_ref, xl_ref, xr_ref, yu_out, yd_out, xu_out, xd_out, c_ref, r_ref, w_ref,
+                yu_ref, yd_ref, xu_ref, xd_ref, sems):
     grad_scales(count, tot_ref, rp_ref, cp_ref, tp_ref, c_ref, r_ref, w_ref)
-    for n, (ref, left, right) in enumerate((
-        (yd_ref, None, yr_ref), (yu_ref, yl_ref, None), (xd_ref, None, xr_ref), (xu_ref, xl_ref, None)
+    yu_ref[256:264, :] = yl_ref[128:136, :]
+    copies = []
+    for n, (ref, left, right, target) in enumerate((
+        (yd_ref, None, yr_ref, yd_out), (yu_ref, yl_ref, None, yu_out),
+        (xd_ref, None, xr_ref, xd_out), (xu_ref, xl_ref, None, xu_out),
     )):
         half, j = LAYOUT[1][n]
         g = grad_block(pos_ref, half, j, k_ref, n * 256, c_ref, r_ref, w_ref)
         out = dot3(g, (ah_ref[...], al_ref[...]), ((1,), (0,)))
         ref[0:128, :] = out[:128] if left is None else out[:128] + left[0:128, :]
         ref[128:256, :] = out[128:] if right is None else out[128:] + right[0:128, :]
-    yu_ref[256:264, :] = yl_ref[128:136, :]
+        copies.append(pltpu.make_async_copy(ref, target, sems.at[n]))
+        copies[n].start()
+    for copy in copies:
+        copy.wait()
 
 
 def own_kernel(count, pos_ref, tot_ref, rp_ref, cp_ref, tp_ref, k_ref, ah_ref, al_ref,
@@ -332,14 +362,17 @@
     row = lax.axis_index("row")
     pos = jnp.stack([row // 4, row % 4]).astype(jnp.int32)
     audio_unit, vt, vb = call(
-        unit_kernel, "unit_rows", [f32(128, 768), f32(64, 768), f32(64, 768)], audio, video
+        unit_kernel, "unit_rows", [f32(128, 768), f32(64, 768), f32(64, 768)],
+        *(pltpu.with_memory_space_constraint(a, pltpu.HBM) for a in (audio, video)),
     )
     audio_tile = lax.all_gather(audio_unit, "col", axis=0, tiled=True)
     join = lambda half, *parts: call(
-        lambda *refs: join_kernel(half, *refs), "join", [f32(256, 768)], *parts, pos=pos, mib=4
+        lambda *refs: join_kernel(half, *refs), "join", [f32(256, 768)], *parts, pos=pos, mib=4,
+        far_out=True, scratch=[pltpu.SemaphoreType.DMA((4,))],
     )[0]
     xl, xr, yl, yr = step_x(vt, 1), step_x(vt, -1), step_y(vb, 1), step_y(vb, -1)
-    first = join(0, vt, xl, xr, step_x(vt, 2))
+    yr, xl, xr = lax.optimization_barrier((yr, xl, xr))
+    first = join(0, vt, xl, xr, step_x(xl, 1))
     second = join(1, vb, yl, yr, step_y(yr, -1))
     fl, fr, sl, sr = step_y(first, 1), step_y(first, -1), step_x(second, 1), step_x(second, -1)
     flops = 3 * 2 * 1024 * 768
@@ -348,10 +381,11 @@
         [bf16(1024, 768), bf16(1024, 768), f32(512, 1024), bf16(512, 768), bf16(512, 768), f32(8, 1024)],
         audio_tile, first, second, flops=512 * flops,
     )
-    fl, fr, sl, sr, sums = lax.optimization_barrier((fl, fr, sl, sr, sums))
     halves = lambda left, right: call(halves_kernel, "halves", [f32(128, 768)] * 2, left, right, mib=4)
+    sl, sr, sums = lax.optimization_barrier((sl, sr, sums))
+    c, d = halves(sl, sr)
+    fl, fr, c = lax.optimization_barrier((fl, fr, c))
     a, b = halves(fl, fr)
-    c, d = halves(sl, sr)
     far = (step_y(a, 1), step_y(b, -1), step_x(c, 1), step_x(d, -1))
     k2, h2, l2, sums = call(
         scores_near_kernel, "scores_near",
@@ -385,19 +419,22 @@
     after, yu = lax.optimization_barrier((tpart, yu))
     yl, yr, xl, xr = step_y(yu, 1), step_y(yd, -1), step_x(xu, 1), step_x(xd, -1)
     (half_audio,) = call(
-        bind(audio_first_kernel), "audio_first", [f32(1024, 768)], totals, rpart, cpart, after, k1, k3,
-        h1, l1, h3, l3, pos=pos, scratch=SCALES, flops=1024 * flops,
+        bind(audio_first_kernel), "audio_first", [f32(1024, 768)], totals, rpart, cpart, after, *ks,
+        h1, l1, h2, l2, h3, l3, pos=pos, scratch=SCALES, flops=1024 * flops,
     )
     yl, yr, xl, xr, half_audio = lax.optimization_barrier((yl, yr, xl, xr, half_audio))
     yu, yd, xu, xd = call(
         bind(near_kernel), "video_near", [f32(264, 768), block, block, block],
-        *vectors, k2, ah, al, yl, yr, xl, xr, pos=pos, scratch=SCALES, flops=1024 * flops,
+        *vectors, k2, ah, al, yl, yr, xl, xr, pos=pos, flops=1024 * flops, mib=12, far_out=True,
+        scratch=SCALES + [pltpu.VMEM((264, 768), F32)] + [pltpu.VMEM((256, 768), F32)] * 3
+        + [pltpu.SemaphoreType.DMA((4,))],
     )
     yu, yd, xu, xd, half_audio = lax.optimization_barrier((yu, yd, xu, xd, half_audio))
     yu, yd, xu, xd = step_y(yu, 1), step_y(yd, -1), step_x(xu, 1), step_x(xd, -1)
     (full_audio,) = call(
         bind(audio_second_kernel), "audio_second", [f32(1024, 768)], *vectors, k2, h2, l2, half_audio,
-        pos=pos, scratch=SCALES, flops=1024 * flops,
+        pos=pos, scratch=SCALES + [pltpu.VMEM((1024, 768), F32), pltpu.SemaphoreType.DMA((4,))],
+        flops=1024 * flops, mib=12, far_out=True,
     )
     unit_audio = lax.psum_scatter(full_audio, "col", scatter_dimension=0, tiled=True)
     after, full_audio = lax.optimization_barrier((tpart, full_audio))
@@ -413,6 +450,7 @@
     )
     y1, y2, y3 = step_x(y1, 1), step_x(y2, 2), step_x(y3, 3)
     x1, x2, x3 = step_y(x1, 1), step_y(x2, 2), step_y(x3, 3)
+    unit_audio, x1 = lax.optimization_barrier((unit_audio, x1))
     (audio_grad,) = call(audio_project_kernel, "audio_grad", [f32(128, 768)], audio, unit_audio)
     video_grad, loss = call(
         bind(video_kernel), "video_grad", [f32(128, 768), f32(1, 1)],

time: 243 us -> 237 us (0.975)
  local copies, waits for them, and re-layouts: 13 us -> 7.98 us
  Pallas kernels: 56.4 us -> 60.1 us
  starting transfers between devices: 45.1 us -> 41.7 us
  waiting for transfers between devices: 33.8 us -> 31.1 us
    ppermute x14, waiting for transfers between devices: 14.3 us -> 8.11 us  [step_x(): lax.ppermute(v, 'row', [(i, i // 4 * 4 + (i % 4 + k) % 4) for i in range(...]
    unnamed x30 -> x20, local copies, waits for them, and re-layouts: 13 us -> 7.98 us
    pallas_call x22, Pallas kernels: 56.4 us -> 60.1 us  [call(): pl.pallas_call(kernel, out_shape=[pltpu.HBM(o.shape, o.dtype) if far_out...]
    ppermute x14, waiting for transfers between devices: 14.3 us -> 17.2 us  [step_y(): lax.ppermute(v, 'row', [(i, (i // 4 + k) % 4 * 4 + i % 4) for i in range(...]
  transfers between devices with their start and end apart: 30 -> 30, of which waited for: 11 -> 14; matrix products, arithmetic and copies ran while one was open for 0% -> 0% of each run, Pallas kernels for 11% -> 12%
where the time goes in v3:
time: 237 us; the launch traced here: 236 us
  blocking collectives  80 us (34%)
  Pallas kernels  60.1 us (25%)
  starting transfers between devices  41.7 us (18%)
  waiting for transfers between devices  31.1 us (13%)
  between operations  14.6 us (6%)
  local copies, waits for them, and re-layouts  7.98 us (3%)
    all_to_all x7, blocking collectives, swap(): return lax.all_to_all(part, axis, 0, 0, tiled=True)  80 us
    pallas_call x22, Pallas kernels, call(): pl.pallas_call(kernel, out_shape=[pltpu.HBM(o.shape, o.dtype) if far_out...  60.1 us
    ppermute x14, starting transfers between devices, step_x(): lax.ppermute(v, 'row', [(i, i // 4 * 4 + (i % 4 + k) % 4) for i in range(...  22.7 us
    ppermute x14, starting transfers between devices, step_y(): lax.ppermute(v, 'row', [(i, (i // 4 + k) % 4 * 4 + i % 4) for i in range(...  18.9 us
    ppermute x14, waiting for transfers between devices, step_y(): lax.ppermute(v, 'row', [(i, (i // 4 + k) % 4 * 4 + i % 4) for i in range(...  17.2 us
    ppermute x14, waiting for transfers between devices, step_x(): lax.ppermute(v, 'row', [(i, i // 4 * 4 + (i % 4 + k) % 4) for i in range(...  8.11 us
    unnamed x20, local copies, waits for them, and re-layouts  7.98 us
    all_gather x1, waiting for transfers between devices, local(): audio_tile = lax.all_gather(audio_unit, 'col', axis=0, tiled=True)  5.47 us
  transfers between devices with their start and end apart: 30, of which 14 were waited for; matrix products, arithmetic and copies ran while one was open for 0% of the time, Pallas kernels for 12%

profile of v3, /device:TPU:0, one launch (start us, length us, event | category | flops | bytes accessed | tf_op | source)
XLA Modules:
  0.0 235.5 jit_solution(117418722622257653)
XLA Ops:
  9.3 3.2 %collective-permute-start = (f32[64,768]{1,0:T(8,128)S(1)}, f32[64,768]{1,0:T(8,128)S(1)}, u32[]{:S(2)}, u32[]{:S(2)}) collective-permute-start(f32[64,768]{1,0:T(8,128)S(1)} %get-tuple-element.75.refs_1_), channel_id=1, source_target_pairs={{0,96},{8,104},{16,112},{24,120},{32,0},{40,8},{48,16},{56,24},{64... | collective-permute-start | bytes 589832 | tf_op jit(solution)/shard_map/ppermute | solution.py:348
  16.6 3.4 %collective-permute-done.1.refs_2_ = f32[64,768]{1,0:T(8,128)S(1)} collective-permute-done((f32[64,768]{1,0:T(8,128)S(1)}, f32[64,768]{1,0:T(8,128)S(1)}, u32[]{:S(2)}, u32[]{:S(2)}) %collective-permute-start.1) | collective-permute-done | bytes 196640 | tf_op jit(solution)/shard_map/ppermute | solution.py:352
  22.7 3.0 %collective-permute-done.5.refs_4_ = f32[64,768]{1,0:T(8,128)S(1)} collective-permute-done((f32[64,768]{1,0:T(8,128)S(1)}, f32[64,768]{1,0:T(8,128)S(1)}, u32[]{:S(2)}, u32[]{:S(2)}) %collective-permute-start.5) | collective-permute-done | bytes 196640 | tf_op jit(solution)/shard_map/ppermute | solution.py:348
  32.0 3.2 %collective-permute-start.9 = (f32[256,768]{1,0:T(8,128)}, f32[256,768]{1,0:T(8,128)}, u32[]{:S(2)}, u32[]{:S(2)}) collective-permute-start(f32[256,768]{1,0:T(8,128)} %join.2.p_ref), channel_id=1, source_target_pairs={{0,96},{8,104},{16,112},{24,120},{32,0},{40,8},{48,16},{56,24},{64... | collective-permute-start | bytes 2359304 | tf_op jit(solution)/shard_map/ppermute | solution.py:348
  35.3 5.5 %all-gather.2.cloned.1.call-done.a_ref = f32[1024,768]{1,0:T(8,128)} async-done(((f32[128,768]{1,0:T(8,128)}), f32[1024,768]{1,0:T(8,128)}) %all-gather.2.cloned.1.call-update) | async-done | bytes 3145744 | tf_op jit(solution)/shard_map/all_gather | solution.py:368
  58.2 6.8 %scores_near.1 = (f32[1024,1024]{1,0:T(8,128)S(1)}, bf16[1024,768]{1,0:T(8,128)(2,1)S(1)}, bf16[1024,768]{1,0:T(8,128)(2,1)S(1)}, f32[8,1024]{1,0:T(8,128)S(1)}) custom-call(bf16[1024,768]{1,0:T(8,128)(2,1)S(1)} %get-tuple-element.79.ah_ref.refs_6_, bf16[1024,768]{1,0:T(8,128)(2,1)S(1)} %get-tuple-element.80.al_ref.refs_7_, ...), custom_call_target="tpu_custom_call" | custom-call | flops 4831838208 | bytes 13697024 | tf_op jit(solution)/shard_map/scores_near/pallas_call | solution.py:39
  69.1 9.6 %all_to_all.35.part_ref.tot_ref.refs_1_ = f32[8,8,128]{2,1,0:T(8,128)S(1)} all-to-all(f32[8,8,128]{2,1,0:T(8,128)S(1)} %get-tuple-element.93), channel_id=1, replica_groups=mesh['row'=16,'col'=8] {'col'}, dimensions={0} | all-to-all | bytes 65536 | tf_op jit(solution)/shard_map/all_to_all | solution.py:356
  79.9 12.5 %all_to_all.36.part_ref = f32[16,16,128]{2,1,0:T(8,128)S(1)} all-to-all(f32[16,16,128]{2,1,0:T(8,128)S(1)} %column_sums.3), channel_id=1, replica_groups=mesh['row'=16,'col'=8] {'row'}, dimensions={0} | all-to-all | bytes 262144 | tf_op jit(solution)/shard_map/all_to_all | solution.py:356
  93.6 7.8 %all_to_all.37.part_ref = f32[8,8,128]{2,1,0:T(8,128)S(1)} all-to-all(f32[8,8,128]{2,1,0:T(8,128)S(1)} %row_sums.2), channel_id=1, replica_groups=mesh['row'=16,'col'=8] {'col'}, dimensions={0} | all-to-all | bytes 65536 | tf_op jit(solution)/shard_map/all_to_all | solution.py:356
  102.6 11.1 %all_to_all.38.part_ref = f32[16,16,128]{2,1,0:T(8,128)S(1)} all-to-all(f32[16,16,128]{2,1,0:T(8,128)S(1)} %column_sums.4), channel_id=1, replica_groups=mesh['row'=16,'col'=8] {'row'}, dimensions={0} | all-to-all | bytes 262144 | tf_op jit(solution)/shard_map/all_to_all | solution.py:356
  114.9 7.8 %all_to_all.39.part_ref.rpart_ref.refs_2_ = f32[8,8,128]{2,1,0:T(8,128)S(1)} all-to-all(f32[8,8,128]{2,1,0:T(8,128)S(1)} %row_sums.3), channel_id=1, replica_groups=mesh['row'=16,'col'=8] {'col'}, dimensions={0} | all-to-all | bytes 65536 | tf_op jit(solution)/shard_map/all_to_all | solution.py:356
  123.9 23.2 %all_to_all.40.part_ref.refs_3_ = f32[16,16,128]{2,1,0:T(8,128)S(1)} all-to-all(f32[16,16,128]{2,1,0:T(8,128)S(1)} %column_sums.5), channel_id=1, replica_groups=mesh['row'=16,'col'=8] {'row'}, dimensions={0} | all-to-all | bytes 262144 | tf_op jit(solution)/shard_map/all_to_all | solution.py:356
  149.4 8.0 %all_to_all.41.refs_4_.tp_ref = f32[8,16,128]{2,1,0:T(8,128)S(1)} all-to-all(f32[8,16,128]{2,1,0:T(8,128)S(1)} %row_sums_and_loss.1), channel_id=1, replica_groups=mesh['row'=16,'col'=8] {'col'}, dimensions={0} | all-to-all | bytes 131072 | tf_op jit(solution)/shard_map/all_to_all | solution.py:356
  157.4 3.4 %video_far.1 = (f32[136,768]{1,0:T(8,128)S(1)}, f32[136,768]{1,0:T(8,128)S(1)}, f32[128,768]{1,0:T(8,128)S(1)}, f32[128,768]{1,0:T(8,128)S(1)}) custom-call(s32[2]{0:T(128)S(1)} %pad_add_fusion.refs_0_.pos_ref, f32[8,8,128]{2,1,0:T(8,128)S(1)} %all_to_all.35.part_ref.tot_ref.refs_1_, f32[8,8,128]{2,1,0:T(8,128)S(1)} %all_to_all.39.part_ref.rpart_ref.refs_2_, ...), custom_call_target="tpu_custom_call" | custom-call | flops 2415919104 | bytes 7127048 | tf_op jit(solution)/shard_map/video_far/pallas_call | solution.py:39
  161.1 3.0 %collective-permute-start.15 = (f32[136,768]{1,0:T(8,128)S(1)}, f32[136,768]{1,0:T(8,128)S(1)}, u32[]{:S(2)}, u32[]{:S(2)}) collective-permute-start(f32[136,768]{1,0:T(8,128)S(1)} %get-tuple-element.99), channel_id=1, source_target_pairs={{0,96},{8,104},{16,112},{24,120},{32,0},{40,8},{48,16},{56,24},{64... | collective-permute-start | bytes 1253384 | tf_op jit(solution)/shard_map/ppermute | solution.py:348
  167.3 8.4 %audio_first.1.refs_8_ = f32[1024,768]{1,0:T(8,128)S(1)} custom-call(s32[2]{0:T(128)S(1)} %pad_add_fusion.refs_0_.pos_ref, f32[8,8,128]{2,1,0:T(8,128)S(1)} %all_to_all.35.part_ref.tot_ref.refs_1_, f32[8,8,128]{2,1,0:T(8,128)S(1)} %all_to_all.39.part_ref.rpart_ref.refs_2_, f32[16,16,128]{2,1,0:T(8,128)S(1)} %all_to_all.40.part_ref.refs_3_, ...), custom_call_target="tpu_custom_call" | custom-call | flops 4831838208 | bytes 18087944 | tf_op jit(solution)/shard_map/audio_first/pallas_call | solution.py:39
  175.7 7.3 %video_near.1 = (f32[264,768]{1,0:T(8,128)}, f32[256,768]{1,0:T(8,128)}, f32[256,768]{1,0:T(8,128)}, f32[256,768]{1,0:T(8,128)}) custom-call(s32[2]{0:T(128)S(1)} %pad_add_fusion.refs_0_.pos_ref, f32[8,8,128]{2,1,0:T(8,128)S(1)} %all_to_all.35.part_ref.tot_ref.refs_1_, f32[8,8,128]{2,1,0:T(8,128)S(1)} %all_to_all.39.part_ref.rpart_ref.refs_2_, ...), custom_call_target="tpu_custom_call" | custom-call | flops 4831838208 | bytes 12394504 | tf_op jit(solution)/shard_map/video_near/pallas_call | solution.py:39
  183.0 4.9 %audio_second.1 = f32[1024,768]{1,0:T(8,128)} custom-call(s32[2]{0:T(128)S(1)} %pad_add_fusion.refs_0_.pos_ref, f32[8,8,128]{2,1,0:T(8,128)S(1)} %all_to_all.35.part_ref.tot_ref.refs_1_, f32[8,8,128]{2,1,0:T(8,128)S(1)} %all_to_all.39.part_ref.rpart_ref.refs_2_, f32[16,16,128]{2,1,0:T(8,128)S(1)} %all_to_all.40.part_ref.refs_3_, ...), custom_call_target="tpu_custom_call" | custom-call | flops 4831838208 | bytes 13893640 | tf_op jit(solution)/shard_map/audio_second/pallas_call | solution.py:39
  188.0 3.2 %collective-permute-start.19 = (f32[256,768]{1,0:T(8,128)}, f32[256,768]{1,0:T(8,128)S(1)}, u32[]{:S(2)}, u32[]{:S(2)}) collective-permute-start(f32[256,768]{1,0:T(8,128)} %get-tuple-element.119), channel_id=1, source_target_pairs={{0,96},{8,104},{16,112},{24,120},{32,0},{40,8},{48,16},{56,24},{64... | collective-permute-start | bytes 2359304 | tf_op jit(solution)/shard_map/ppermute | solution.py:348
  191.3 3.2 %collective-permute-start.21 = (f32[256,768]{1,0:T(8,128)}, f32[256,768]{1,0:T(8,128)S(1)}, u32[]{:S(2)}, u32[]{:S(2)}) collective-permute-start(f32[256,768]{1,0:T(8,128)} %get-tuple-element.121), channel_id=1, source_target_pairs={{0,24},{8,0},{16,8},{24,16},{32,56},{40,32},{48,40},{56,48},{64,88... | collective-permute-start | bytes 2359304 | tf_op jit(solution)/shard_map/ppermute | solution.py:352
  197.3 3.5 %video_own.1 = (f32[256,768]{1,0:T(8,128)S(1)}, f32[256,768]{1,0:T(8,128)S(1)}) custom-call(s32[2]{0:T(128)S(1)} %pad_add_fusion.refs_0_.pos_ref, f32[8,8,128]{2,1,0:T(8,128)S(1)} %all_to_all.35.part_ref.tot_ref.refs_1_, f32[8,8,128]{2,1,0:T(8,128)S(1)} %all_to_all.39.part_ref.rpart_ref.refs_2_, f32[16,16,128]{2,1,0:T(8,128)S(1)} %all_to_all.40.part_ref.refs_3_, ...), custom_call_target="tpu_custom_call" | custom-call | flops 2415919104 | bytes 7077896 | tf_op jit(solution)/shard_map/video_own/pallas_call | solution.py:39
  200.8 6.1 %collective-permute-done.19.yd_ref = f32[256,768]{1,0:T(8,128)S(1)} collective-permute-done((f32[256,768]{1,0:T(8,128)}, f32[256,768]{1,0:T(8,128)S(1)}, u32[]{:S(2)}, u32[]{:S(2)}) %collective-permute-start.19) | collective-permute-done | bytes 786464 | tf_op jit(solution)/shard_map/ppermute | solution.py:348
  206.9 3.3 %collective-permute-done.20.xu_ref = f32[256,768]{1,0:T(8,128)S(1)} collective-permute-done((f32[256,768]{1,0:T(8,128)}, f32[256,768]{1,0:T(8,128)S(1)}, u32[]{:S(2)}, u32[]{:S(2)}) %collective-permute-start.20) | collective-permute-done | bytes 786464 | tf_op jit(solution)/shard_map/ppermute | solution.py:352
  212.2 4.2 %collective-permute-start.23 = (f32[72,768]{1,0:T(8,128)}, f32[72,768]{1,0:T(8,128)S(1)}, u32[]{:S(2)}, u32[]{:S(2)}) collective-permute-start(f32[72,768]{1,0:T(8,128)} %get-tuple-element.133), channel_id=1, source_target_pairs={{0,16},{8,24},{16,0},{24,8},{32,48},{40,56},{48,32},{56,40},{64,80... | collective-permute-start | bytes 663560 | tf_op jit(solution)/shard_map/ppermute | solution.py:352
  (88 shorter events, 65.5 us)
Async XLA Ops:
  7.2 33.6 %all-gather.2.cloned.1.call-start = ((), (), s32[]{:S(2)}) async-start(), calls=%async_computation.8 | async-start | bytes 3538944 | tf_op jit(solution)/shard_map/all_gather | solution.py:368
  9.2 212.1 %reduce-scatter.2.cloned.1.call-start = ((), (), s32[]{:S(2)}) async-start(), calls=%async_computation.9 | async-start | bytes 3538944 | tf_op jit(solution)/shard_map/reduce_scatter | solution.py:439
  12.4 7.6 %collective-permute-start.1 = (f32[64,768]{1,0:T(8,128)S(1)}, f32[64,768]{1,0:T(8,128)S(1)}, u32[]{:S(2)}, u32[]{:S(2)}) collective-permute-start(f32[64,768]{1,0:T(8,128)S(1)} %get-tuple-element.74.refs_1_), channel_id=1, source_target_pairs={{0,8},{8,16},{16,24},{24,0},{32,40},{40,48},{48,56},{56,32},{64,72... | collective-permute-start | bytes 589832 | tf_op jit(solution)/shard_map/ppermute | solution.py:352
  20.7 9.7 %collective-permute-start.3 = (f32[64,768]{1,0:T(8,128)S(1)}, f32[64,768]{1,0:T(8,128)S(1)}, u32[]{:S(2)}, u32[]{:S(2)}) collective-permute-start(f32[64,768]{1,0:T(8,128)S(1)} %collective-permute-done.1.refs_2_), channel_id=1, source_target_pairs={{0,8},{8,16},{16,24},{24,0},{32,40},{40,48},{48,56},{56,32},{64,72... | collective-permute-start | bytes 589832 | tf_op jit(solution)/shard_map/ppermute | solution.py:352
  27.2 20.4 %collective-permute-start.6 = (f32[256,768]{1,0:T(8,128)}, f32[256,768]{1,0:T(8,128)S(1)}, u32[]{:S(2)}, u32[]{:S(2)}) collective-permute-start(f32[256,768]{1,0:T(8,128)} %join.3.q_ref), channel_id=1, source_target_pairs={{0,8},{8,16},{16,24},{24,0},{32,40},{40,48},{48,56},{56,32},{64,72... | collective-permute-start | bytes 2359304 | tf_op jit(solution)/shard_map/ppermute | solution.py:352
  28.7 18.9 %collective-permute-start.7 = (f32[256,768]{1,0:T(8,128)}, f32[256,768]{1,0:T(8,128)}, u32[]{:S(2)}, u32[]{:S(2)}) collective-permute-start(f32[256,768]{1,0:T(8,128)} %join.3.q_ref), channel_id=1, source_target_pairs={{0,24},{8,0},{16,8},{24,16},{32,56},{40,32},{48,40},{56,48},{64,88... | collective-permute-start | bytes 2359304 | tf_op jit(solution)/shard_map/ppermute | solution.py:352
  32.0 18.0 %collective-permute-start.8 = (f32[256,768]{1,0:T(8,128)}, f32[256,768]{1,0:T(8,128)}, u32[]{:S(2)}, u32[]{:S(2)}) collective-permute-start(f32[256,768]{1,0:T(8,128)} %join.2.p_ref), channel_id=1, source_target_pairs={{0,32},{8,40},{16,48},{24,56},{32,64},{40,72},{48,80},{56,88},{64,... | collective-permute-start | bytes 2359304 | tf_op jit(solution)/shard_map/ppermute | solution.py:348
  32.0 17.9 %collective-permute-start.9 = (f32[256,768]{1,0:T(8,128)}, f32[256,768]{1,0:T(8,128)}, u32[]{:S(2)}, u32[]{:S(2)}) collective-permute-start(f32[256,768]{1,0:T(8,128)} %join.2.p_ref), channel_id=1, source_target_pairs={{0,96},{8,104},{16,112},{24,120},{32,0},{40,8},{48,16},{56,24},{64... | collective-permute-start | bytes 2359304 | tf_op jit(solution)/shard_map/ppermute | solution.py:348
  51.4 13.7 %collective-permute-start.10 = (f32[128,768]{1,0:T(8,128)S(1)}, f32[128,768]{1,0:T(8,128)S(1)}, u32[]{:S(2)}, u32[]{:S(2)}) collective-permute-start(f32[128,768]{1,0:T(8,128)S(1)} %get-tuple-element.89), channel_id=1, source_target_pairs={{0,32},{8,40},{16,48},{24,56},{32,64},{40,72},{48,80},{56,88},{64,... | collective-permute-start | bytes 1179656 | tf_op jit(solution)/shard_map/ppermute | solution.py:348
  52.4 12.6 %collective-permute-start.11 = (f32[128,768]{1,0:T(8,128)S(1)}, f32[128,768]{1,0:T(8,128)S(1)}, u32[]{:S(2)}, u32[]{:S(2)}) collective-permute-start(f32[128,768]{1,0:T(8,128)S(1)} %get-tuple-element.90), channel_id=1, source_target_pairs={{0,96},{8,104},{16,112},{24,120},{32,0},{40,8},{48,16},{56,24},{64... | collective-permute-start | bytes 1179656 | tf_op jit(solution)/shard_map/ppermute | solution.py:348
  54.7 11.4 %collective-permute-start.12 = (f32[128,768]{1,0:T(8,128)S(1)}, f32[128,768]{1,0:T(8,128)S(1)}, u32[]{:S(2)}, u32[]{:S(2)}) collective-permute-start(f32[128,768]{1,0:T(8,128)S(1)} %get-tuple-element.91), channel_id=1, source_target_pairs={{0,8},{8,16},{16,24},{24,0},{32,40},{40,48},{48,56},{56,32},{64,72... | collective-permute-start | bytes 1179656 | tf_op jit(solution)/shard_map/ppermute | solution.py:352
  55.6 10.8 %collective-permute-start.13 = (f32[128,768]{1,0:T(8,128)S(1)}, f32[128,768]{1,0:T(8,128)S(1)}, u32[]{:S(2)}, u32[]{:S(2)}) collective-permute-start(f32[128,768]{1,0:T(8,128)S(1)} %get-tuple-element.92), channel_id=1, source_target_pairs={{0,24},{8,0},{16,8},{24,16},{32,56},{40,32},{48,40},{56,48},{64,88... | collective-permute-start | bytes 1179656 | tf_op jit(solution)/shard_map/ppermute | solution.py:352
  160.8 14.9 %collective-permute-start.14 = (f32[136,768]{1,0:T(8,128)S(1)}, f32[136,768]{1,0:T(8,128)S(1)}, u32[]{:S(2)}, u32[]{:S(2)}) collective-permute-start(f32[136,768]{1,0:T(8,128)S(1)} %get-tuple-element.98), channel_id=1, source_target_pairs={{0,32},{8,40},{16,48},{24,56},{32,64},{40,72},{48,80},{56,88},{64,... | collective-permute-start | bytes 1253384 | tf_op jit(solution)/shard_map/ppermute | solution.py:348
  161.1 14.6 %collective-permute-start.15 = (f32[136,768]{1,0:T(8,128)S(1)}, f32[136,768]{1,0:T(8,128)S(1)}, u32[]{:S(2)}, u32[]{:S(2)}) collective-permute-start(f32[136,768]{1,0:T(8,128)S(1)} %get-tuple-element.99), channel_id=1, source_target_pairs={{0,96},{8,104},{16,112},{24,120},{32,0},{40,8},{48,16},{56,24},{64... | collective-permute-start | bytes 1253384 | tf_op jit(solution)/shard_map/ppermute | solution.py:348
  164.1 11.6 %collective-permute-start.16 = (f32[128,768]{1,0:T(8,128)S(1)}, f32[128,768]{1,0:T(8,128)S(1)}, u32[]{:S(2)}, u32[]{:S(2)}) collective-permute-start(f32[128,768]{1,0:T(8,128)S(1)} %get-tuple-element.100), channel_id=1, source_target_pairs={{0,8},{8,16},{16,24},{24,0},{32,40},{40,48},{48,56},{56,32},{64,72... | collective-permute-start | bytes 1179656 | tf_op jit(solution)/shard_map/ppermute | solution.py:352
  164.6 11.1 %collective-permute-start.17 = (f32[128,768]{1,0:T(8,128)S(1)}, f32[128,768]{1,0:T(8,128)S(1)}, u32[]{:S(2)}, u32[]{:S(2)}) collective-permute-start(f32[128,768]{1,0:T(8,128)S(1)} %get-tuple-element.101), channel_id=1, source_target_pairs={{0,24},{8,0},{16,8},{24,16},{32,56},{40,32},{48,40},{56,48},{64,88... | collective-permute-start | bytes 1179656 | tf_op jit(solution)/shard_map/ppermute | solution.py:352
  187.9 22.3 %collective-permute-start.18 = (f32[264,768]{1,0:T(8,128)}, f32[264,768]{1,0:T(8,128)S(1)}, u32[]{:S(2)}, u32[]{:S(2)}) collective-permute-start(f32[264,768]{1,0:T(8,128)} %get-tuple-element.118), channel_id=1, source_target_pairs={{0,32},{8,40},{16,48},{24,56},{32,64},{40,72},{48,80},{56,88},{64,... | collective-permute-start | bytes 2433032 | tf_op jit(solution)/shard_map/ppermute | solution.py:348
  188.0 18.9 %collective-permute-start.19 = (f32[256,768]{1,0:T(8,128)}, f32[256,768]{1,0:T(8,128)S(1)}, u32[]{:S(2)}, u32[]{:S(2)}) collective-permute-start(f32[256,768]{1,0:T(8,128)} %get-tuple-element.119), channel_id=1, source_target_pairs={{0,96},{8,104},{16,112},{24,120},{32,0},{40,8},{48,16},{56,24},{64... | collective-permute-start | bytes 2359304 | tf_op jit(solution)/shard_map/ppermute | solution.py:348
  191.2 19.0 %collective-permute-start.20 = (f32[256,768]{1,0:T(8,128)}, f32[256,768]{1,0:T(8,128)S(1)}, u32[]{:S(2)}, u32[]{:S(2)}) collective-permute-start(f32[256,768]{1,0:T(8,128)} %get-tuple-element.120), channel_id=1, source_target_pairs={{0,8},{8,16},{16,24},{24,0},{32,40},{40,48},{48,56},{56,32},{64,72... | collective-permute-start | bytes 2359304 | tf_op jit(solution)/shard_map/ppermute | solution.py:352
  191.3 19.0 %collective-permute-start.21 = (f32[256,768]{1,0:T(8,128)}, f32[256,768]{1,0:T(8,128)S(1)}, u32[]{:S(2)}, u32[]{:S(2)}) collective-permute-start(f32[256,768]{1,0:T(8,128)} %get-tuple-element.121), channel_id=1, source_target_pairs={{0,24},{8,0},{16,8},{24,16},{32,56},{40,32},{48,40},{56,48},{64,88... | collective-permute-start | bytes 2359304 | tf_op jit(solution)/shard_map/ppermute | solution.py:352
  212.0 9.0 %collective-permute-start.25 = (f32[64,768]{1,0:T(8,128)S(1)}, f32[64,768]{1,0:T(8,128)S(1)}, u32[]{:S(2)}, u32[]{:S(2)}) collective-permute-start(f32[64,768]{1,0:T(8,128)S(1)} %get-tuple-element.136), channel_id=1, source_target_pairs={{0,32},{8,40},{16,48},{24,56},{32,64},{40,72},{48,80},{56,88},{64,... | collective-permute-start | bytes 589832 | tf_op jit(solution)/shard_map/ppermute | solution.py:348
  212.0 14.9 %collective-permute-start.22 = (f32[72,768]{1,0:T(8,128)}, f32[72,768]{1,0:T(8,128)S(1)}, u32[]{:S(2)}, u32[]{:S(2)}) collective-permute-start(f32[72,768]{1,0:T(8,128)} %get-tuple-element.132), channel_id=1, source_target_pairs={{0,8},{8,16},{16,24},{24,0},{32,40},{40,48},{48,56},{56,32},{64,72... | collective-permute-start | bytes 663560 | tf_op jit(solution)/shard_map/ppermute | solution.py:352
  212.2 14.7 %collective-permute-start.23 = (f32[72,768]{1,0:T(8,128)}, f32[72,768]{1,0:T(8,128)S(1)}, u32[]{:S(2)}, u32[]{:S(2)}) collective-permute-start(f32[72,768]{1,0:T(8,128)} %get-tuple-element.133), channel_id=1, source_target_pairs={{0,16},{8,24},{16,0},{24,8},{32,48},{40,56},{48,32},{56,40},{64,80... | collective-permute-start | bytes 663560 | tf_op jit(solution)/shard_map/ppermute | solution.py:352
  216.4 10.5 %collective-permute-start.24 = (f32[72,768]{1,0:T(8,128)S(1)}, f32[72,768]{1,0:T(8,128)S(1)}, u32[]{:S(2)}, u32[]{:S(2)}) collective-permute-start(f32[72,768]{1,0:T(8,128)S(1)} %get-tuple-element.134), channel_id=1, source_target_pairs={{0,24},{8,0},{16,8},{24,16},{32,56},{40,32},{48,40},{56,48},{64,88... | collective-permute-start | bytes 663560 | tf_op jit(solution)/shard_map/ppermute | solution.py:352
  (16 other events, 331.5 us)
Sparse Core Ops, SparseCore 0:
  10.3 30.4 all-gather.1
  188.1 33.2 reduce-scatter.1
